TPU v7x, 32 devices: a whole 2x2x4 slice. The times are simulated.
32 devices in a mesh: dp: 2 (over core), seq: 16 (over z, y, x).
Axes of the slice: x: 2, y: 2, z: 4, core: 2. Of those that a mesh axis runs over, the one named last changes fastest.
Arguments:
- tokens: bfloat16 [2, 2, 8192, 768], P(None, 'dp', 'seq'), may hold values from -6 to 6
- in_weight: bfloat16 [768, 3352], P('dp'), may hold values from -0.21875 to 0.21875
- out_weight: bfloat16 [1536, 768], P('dp'), may hold values from -0.15625 to 0.15625
- conv_weight: float32 [4, 1792], replicated, may hold values from -3 to 3
- conv_bias: float32 [1792], replicated, may hold values from -0.5 to 0.5
- norm_gain: float32 [768], replicated, may hold values from 0.5 to 1.5
- out_gain: float32 [1536], replicated, may hold values from 0.5 to 1.5
- skip_gain: float32 [24], replicated, may hold values from 0.5 to 1.5
- rate_code: int32 [24], replicated, may hold values from 0 to 31
- step_code: int32 [24], replicated, may hold values from 0 to 31
- cotangent: bfloat16 [2, 2, 8192, 768], P(None, 'dp', 'seq'), may hold values from -6 to 6
Outputs:
- mixed: bfloat16 [2, 2, 8192, 768], P(None, 'dp', 'seq')
- grad_tokens: bfloat16 [2, 2, 8192, 768], P(None, 'dp', 'seq')
- grad_in_weight: float32 [768, 3352], P('dp')
- grad_out_weight: float32 [1536, 768], P('dp')
- grad_conv_weight: float32 [4, 1792], replicated
- grad_conv_bias: float32 [1792], replicated
- grad_norm_gain: float32 [768], replicated
- grad_out_gain: float32 [1536], replicated
- grad_skip_gain: float32 [24], replicated
- grad_log_rate: float32 [24], replicated
- grad_step_bias: float32 [24], replicated
All inputs are finite; a program needn't handle non-finite values.
Results may differ from a plain program's by a relative error of at most 0.0072.
Values may be sent and summed in bfloat16 or wider, within the bound.
A program may use at most 320 MiB of HBM per device.

v0:
```python
import jax
import jax.numpy as jnp
from jax import lax
from jax.sharding import PartitionSpec as P

D = 768
DIN = 1536
HEADS = 24
HEAD_DIM = 64
STATE = 128
CONV = 4
XBC = 1792
PROJ = 3352


EPS = 1e-05
HIGH = lax.Precision.HIGHEST


def from_behind(value, axis, steps):
    count = lax.axis_size(axis)
    leading, last = (max(0, -steps), min(count, count - steps))
    return lax.ppermute(value, axis, [(source, source + steps) for source in range(leading, last)])


def rms_scale(values):
    return lax.rsqrt(jnp.mean(values * values, axis=-1, keepdims=True) + EPS)


def silu_slope(values):
    sigma = jax.nn.sigmoid(values)
    return sigma * (1.0 + values * (1.0 - sigma))


def link_weights(totals, count, mine, upward):
    rows = jnp.arange(count, dtype=jnp.int32)
    ranks = jnp.arange(totals.shape[0], dtype=jnp.int32)
    lower = jnp.minimum(rows, mine)[:, None]
    upper = jnp.maximum(rows, mine)[:, None]
    inside = ((ranks[None, :] > lower) & (ranks[None, :] < upper)).astype(jnp.float32)
    exponent = jnp.einsum("ck,kgh->cgh", inside, totals, precision=HIGH)
    valid = rows > mine if upward else rows < mine
    return jnp.where(valid[:, None, None], jnp.exp(exponent), 0.0)


def fold_states(totals, mine, upward, piece):
    weights = link_weights(totals, piece.shape[0], mine, upward)
    return jnp.einsum("cgh,cghpn->ghpn", weights, piece, precision=HIGH)


def per_device(
    tokens,
    in_weight,
    out_weight,
    conv_weight,
    conv_bias,
    norm_gain,
    out_gain,
    skip_gain,
    rate_code,
    step_code,
    cotangent,
):
    groups, length = (tokens.shape[1], tokens.shape[2])
    log_rate = -4.0 + 0.25 * rate_code.astype(jnp.float32)
    step_bias = -9.0 + 0.25 * step_code.astype(jnp.float32)
    decay_rate = -jnp.exp(log_rate)
    causal = jnp.tril(jnp.ones((length, length), dtype=bool))
    mine = lax.axis_index("seq")
    grad_in_total = jnp.zeros((D, PROJ), jnp.float32)
    grad_out_total = jnp.zeros((DIN, D), jnp.float32)
    grad_conv_weight = jnp.zeros((CONV, XBC), jnp.float32)
    grad_conv_bias = jnp.zeros((XBC,), jnp.float32)
    grad_norm_gain = jnp.zeros((D,), jnp.float32)
    grad_out_gain = jnp.zeros((DIN,), jnp.float32)
    grad_skip = jnp.zeros((HEADS,), jnp.float32)
    grad_log_rate = jnp.zeros((HEADS,), jnp.float32)
    grad_step_bias = jnp.zeros((HEADS,), jnp.float32)
    outputs = []
    grads = []
    for batch in range(tokens.shape[0]):
        weights_in, weights_out = (
            lax.all_gather(in_weight, "dp", axis=0, tiled=True),
            lax.all_gather(out_weight, "dp", axis=0, tiled=True),
        )
        source = tokens[batch].astype(jnp.float32)
        in_scale = rms_scale(source)
        normed = (source * in_scale * norm_gain).astype(jnp.bfloat16)
        projected = jnp.einsum(
            "gld,dp->glp", normed, weights_in, preferred_element_type=jnp.float32
        )
        gate_in = projected[..., :DIN]
        conv_in = projected[..., DIN : DIN + XBC]
        step_raw = projected[..., DIN + XBC :]
        edge = from_behind(conv_in[:, length - (CONV - 1) :, :], "seq", 1)
        padded = jnp.concatenate([edge, conv_in], axis=1)
        conv_out = conv_bias + sum(
            (conv_weight[k] * padded[:, k : k + length, :] for k in range(CONV))
        )
        mixed_in = jax.nn.silu(conv_out)
        x_heads = mixed_in[..., :DIN].reshape(groups, length, HEADS, HEAD_DIM)
        b_proj = mixed_in[..., DIN : DIN + STATE]
        c_proj = mixed_in[..., DIN + STATE :]
        step_arg = step_raw + step_bias
        step_size = jax.nn.softplus(step_arg)
        log_decay = jnp.cumsum(step_size * decay_rate, axis=1)
        decay_heads = jnp.swapaxes(log_decay, 1, 2)
        step_heads = jnp.swapaxes(step_size, 1, 2)
        gram = jnp.einsum("gtn,gsn->gts", c_proj, b_proj, precision=HIGH)
        gaps = decay_heads[:, :, :, None] - decay_heads[:, :, None, :]
        lower_mat = jnp.where(causal, jnp.exp(jnp.where(causal, gaps, 0.0)), 0.0)
        scored = gram[:, None] * lower_mat
        mixing = scored * step_heads[:, :, None, :]
        y_inner = jnp.einsum("ghts,gshp->gthp", mixing, x_heads, precision=HIGH)
        block_total = log_decay[:, -1, :]
        tail_decay = jnp.exp(block_total[:, None, :] - log_decay)
        tail_weight = tail_decay * step_size
        weighted_x = tail_weight[..., None] * x_heads
        local_state = jnp.einsum("gshp,gsn->ghpn", weighted_x, b_proj, precision=HIGH)
        totals = lax.all_gather(block_total[None], "seq", axis=0, tiled=True)
        start_state = fold_states(
            totals, mine, False, lax.all_gather(local_state[None], "seq", axis=0, tiled=True)
        )
        head_decay = jnp.exp(log_decay)
        carried = jnp.einsum("ghpn,gtn->gthp", start_state, c_proj, precision=HIGH)
        y_state = head_decay[..., None] * carried
        y_heads = y_inner + y_state + skip_gain[:, None] * x_heads
        y_flat = y_heads.reshape(groups, length, DIN)
        gate_act = jax.nn.silu(gate_in)
        gated = y_flat * gate_act
        out_scale = rms_scale(gated)
        branch = (gated * out_scale * out_gain).astype(jnp.bfloat16)
        result = jnp.einsum("glk,kd->gld", branch, weights_out, preferred_element_type=jnp.float32)
        outputs.append((source + result).astype(jnp.bfloat16))
        upstream = cotangent[batch]
        up_float = upstream.astype(jnp.float32)
        grad_out_total = grad_out_total + jnp.einsum(
            "glk,gld->kd", branch, upstream, preferred_element_type=jnp.float32
        )
        d_branch = jnp.einsum(
            "gld,kd->glk", upstream, weights_out, preferred_element_type=jnp.float32
        )
        grad_out_gain = grad_out_gain + jnp.sum(d_branch * gated * out_scale, axis=(0, 1))
        d_norm = d_branch * out_gain
        d_gated = out_scale * d_norm - gated * out_scale**3 * jnp.mean(
            d_norm * gated, axis=-1, keepdims=True
        )
        d_gate_in = d_gated * y_flat * silu_slope(gate_in)
        d_heads = (d_gated * gate_act).reshape(groups, length, HEADS, HEAD_DIM)
        grad_skip = grad_skip + jnp.sum(d_heads * x_heads, axis=(0, 1, 3))
        d_x = skip_gain[:, None] * d_heads
        d_mixing = jnp.einsum("gthp,gshp->ghts", d_heads, x_heads, precision=HIGH)
        d_x = d_x + jnp.einsum("ghts,gthp->gshp", mixing, d_heads, precision=HIGH)
        d_scored = d_mixing * step_heads[:, :, None, :]
        d_step_heads = jnp.sum(d_mixing * scored, axis=2)
        d_gram = jnp.sum(d_scored * lower_mat, axis=1)
        flows = d_scored * scored
        d_decay_heads = jnp.sum(flows, axis=3) - jnp.sum(flows, axis=2)
        d_c = jnp.einsum("gts,gsn->gtn", d_gram, b_proj, precision=HIGH)
        d_b = jnp.einsum("gts,gtn->gsn", d_gram, c_proj, precision=HIGH)
        d_carried = d_heads * head_decay[..., None]
        d_log_decay = jnp.swapaxes(d_decay_heads, 1, 2) + jnp.sum(d_heads * y_state, axis=-1)
        d_start = jnp.einsum("gthp,gtn->ghpn", d_carried, c_proj, precision=HIGH)
        d_c = d_c + jnp.einsum("gthp,ghpn->gtn", d_carried, start_state, precision=HIGH)
        later_grad = fold_states(
            totals, mine, True, lax.all_gather(d_start[None], "seq", axis=0, tiled=True)
        )
        d_total = jnp.exp(block_total) * jnp.sum(later_grad * start_state, axis=(2, 3))
        pulled = jnp.einsum("ghpn,gsn->gshp", later_grad, b_proj, precision=HIGH)
        d_x = d_x + tail_weight[..., None] * pulled
        d_b = d_b + jnp.einsum("gshp,ghpn->gsn", weighted_x, later_grad, precision=HIGH)
        d_tail = jnp.sum(x_heads * pulled, axis=-1)
        d_step = jnp.swapaxes(d_step_heads, 1, 2) + d_tail * tail_decay
        d_spread = d_tail * tail_weight
        d_total = d_total + jnp.sum(d_spread, axis=1)
        d_log_decay = d_log_decay - d_spread
        d_log_decay = d_log_decay.at[:, -1, :].add(d_total)
        d_rate_terms = lax.cumsum(d_log_decay, axis=1, reverse=True)
        d_step = d_step + d_rate_terms * decay_rate
        grad_log_rate = grad_log_rate + jnp.sum(d_rate_terms * step_size, axis=(0, 1)) * decay_rate
        d_arg = d_step * jax.nn.sigmoid(step_arg)
        grad_step_bias = grad_step_bias + jnp.sum(d_arg, axis=(0, 1))
        d_mixed = jnp.concatenate([d_x.reshape(groups, length, DIN), d_b, d_c], axis=-1)
        d_conv = d_mixed * silu_slope(conv_out)
        grad_conv_bias = grad_conv_bias + jnp.sum(d_conv, axis=(0, 1))
        grad_conv_weight = grad_conv_weight + jnp.stack(
            [jnp.sum(d_conv * padded[:, k : k + length, :], axis=(0, 1)) for k in range(CONV)]
        )
        d_padded = sum(
            (
                jnp.pad(conv_weight[k] * d_conv, ((0, 0), (k, CONV - 1 - k), (0, 0)))
                for k in range(CONV)
            )
        )
        returned = from_behind(d_padded[:, : CONV - 1, :], "seq", -1)
        d_conv_in = d_padded[:, CONV - 1 :, :] + jnp.pad(
            returned, ((0, 0), (length - (CONV - 1), 0), (0, 0))
        )
        d_projected = jnp.concatenate([d_gate_in, d_conv_in, d_arg], axis=-1).astype(jnp.bfloat16)
        grad_in_total = grad_in_total + jnp.einsum(
            "gld,glp->dp", normed, d_projected, preferred_element_type=jnp.float32
        )
        d_normed = jnp.einsum(
            "glp,dp->gld", d_projected, weights_in, preferred_element_type=jnp.float32
        )
        grad_norm_gain = grad_norm_gain + jnp.sum(d_normed * source * in_scale, axis=(0, 1))
        d_unit = d_normed * norm_gain
        d_source = in_scale * d_unit - source * in_scale**3 * jnp.mean(
            d_unit * source, axis=-1, keepdims=True
        )
        grads.append((up_float + d_source).astype(jnp.bfloat16))
    rows_in, rows_out = (
        lax.psum_scatter(grad_in_total, "dp", scatter_dimension=0, tiled=True),
        lax.psum_scatter(grad_out_total, "dp", scatter_dimension=0, tiled=True),
    )
    share_in, share_out = lax.psum((rows_in, rows_out), "seq")
    summed = lax.psum(
        (
            grad_conv_weight,
            grad_conv_bias,
            grad_norm_gain,
            grad_out_gain,
            grad_skip,
            grad_log_rate,
            grad_step_bias,
        ),
        ("dp", "seq"),
    )
    return (
        jnp.stack(outputs),
        jnp.stack(grads),
        share_in,
        share_out,
        summed[0],
        summed[1],
        summed[2],
        summed[3],
        summed[4],
        summed[5],
        summed[6],
    )


def solution(mesh):
    placed = (
        P(None, "dp", "seq", None),
        P("dp", None),
        P("dp", None),
        P(),
        P(),
        P(),
        P(),
        P(),
        P(),
        P(),
        P(None, "dp", "seq", None),
    )
    return jax.shard_map(
        per_device,
        mesh=mesh,
        in_specs=placed,
        out_specs=(
            P(None, "dp", "seq", None),
            P(None, "dp", "seq", None),
            P("dp", None),
            P("dp", None),
            P(),
            P(),
            P(),
            P(),
            P(),
            P(),
            P(),
        ),
        check_vma=False,
    )
```

profile of v0, /device:TPU:0, one launch (start us, length us, event | category | flops | bytes accessed | tf_op | source)
XLA Modules:
  0.0 1270.6 jit_solution(16758070498587012477)
XLA Ops:
  10.5 16.8 %all-gather.11.cloned.1.call-done = bf16[768,3352]{0,1:T(8,128)(2,1)} async-done(((bf16[384,3352]{0,1:T(8,128)(2,1)}), bf16[768,3352]{0,1:T(8,128)(2,1)}) %all-gather.11.cloned.1.call-update) | async-done | bytes 5148688 | tf_op jit(solution)/shard_map/all_gather | solution.py:83
  68.7 15.9 %fusion.57 = (f32[1,512,1792]{2,1,0:T(8,128)S(1)}, f32[1,512,1792]{2,1,0:T(8,128)}, f32[1,512,1792]{2,1,0:T(8,128)}, f32[1,512,1792]{2,1,0:T(8,128)}) fusion(f32[1,512,1792]{2,1,0:T(8,128)} %slice.235, f32[1792]{0:T(1024)} %get-tuple-element.77, f32[1,3,1792]{2,1,0:T(4,128)S(1)} %copy.288, f32[1792]{0:T(1024)} %get-tuple-element.78, ...), kind=kLoop, calls=%fused_computation.86 | loop fusion | flops 27525120 | bytes 22098944 | tf_op jit(solution)/shard_map/jit(silu)/mul | solution.py:100
  124.7 36.8 %all_gather.27 = f32[16,1,24]{2,1,0:T(1,128)S(1)} all-gather(f32[1,1,24]{2,1,0:T(1,128)} %get-tuple-element.141), channel_id=1, replica_groups=mesh['dp'=2,'seq'=16] {'seq'}, dimensions={0}, use_global_device_ids=true | all-gather | bytes 1632 | tf_op jit(solution)/shard_map/all_gather | solution.py:120
  161.5 36.5 %all_gather.30 = f32[16,1,24]{2,1,0:T(1,128)S(1)} all-gather(f32[1,1,24]{2,1,0:T(1,128)} %get-tuple-element.143), channel_id=1, replica_groups=mesh['dp'=2,'seq'=16] {'seq'}, dimensions={0}, use_global_device_ids=true | all-gather | bytes 1632 | tf_op jit(solution)/shard_map/all_gather | solution.py:120
  220.4 26.9 %all-gather.15.cloned.1.call-done = f32[384,64,128]{2,1,0:T(8,128)} async-done(((f32[24,64,128]{2,1,0:T(8,128)}), f32[384,64,128]{2,1,0:T(8,128)}) %all-gather.15.cloned.1.call-update) | async-done | bytes 12582928 | tf_op jit(solution)/shard_map/all_gather | solution.py:122
  247.4 18.3 %fusion.24 = f32[24,1,64,128]{3,1,2,0:T(1,128)S(1)} fusion(f32[16,24,1,1]{0,2,3,1:T(1,128)} %copy.355, f32[16,24,64,128]{3,2,1,0:T(8,128)} %bitcast.554), kind=kOutput, calls=%fused_computation.26 | convolution fusion | flops 37748736 | bytes 13370880 | tf_op jit(solution)/shard_map/cgh,cghpn->ghpn/dot_general | solution.py:48
  269.6 30.9 %fusion.61 = f32[1,512,24,64]{1,3,2,0:T(8,128)} fusion(f32[1,512,24,64]{1,3,2,0:T(8,128)S(1)} %bitcast.542, f32[512,24,64]{0,2,1:T(8,128)S(1)} %fusion.169, f32[512,24,64]{0,2,1:T(8,128)S(1)} %bitcast.543, f32[24,512]{1,0:T(8,128)S(1)} %copy-done.92, f32[24,512]{1,0:T(8,128)S(1)} %copy-done.97, f32[512,512]{1,0:T(8,128)S(1)} %copy-done.67, ...), kind=kOutput, calls=%fused_computation.97 | convolution fusion | flops 4866441216 | bytes 14041184 | tf_op jit(solution)/shard_map/ghts,gshp->gthp/dot_general | solution.py:114
  304.3 96.5 %all-gather.17.cloned.1.call-done = f32[384,64,128]{2,1,0:T(8,128)} async-done(((f32[24,64,128]{2,1,0:T(8,128)}), f32[384,64,128]{2,1,0:T(8,128)}) %all-gather.17.cloned.1.call-update) | async-done | bytes 12582928 | tf_op jit(solution)/shard_map/all_gather | solution.py:122
  400.8 18.2 %fusion.22 = f32[24,1,64,128]{3,1,2,0:T(1,128)S(1)} fusion(f32[16,24,1,1]{0,2,3,1:T(1,128)} %copy.359, f32[16,24,64,128]{3,2,1,0:T(8,128)} %bitcast.555), kind=kOutput, calls=%fused_computation.24 | convolution fusion | flops 37748736 | bytes 13370880 | tf_op jit(solution)/shard_map/cgh,cghpn->ghpn/dot_general | solution.py:48
  423.1 31.1 %fusion.60 = f32[1,512,24,64]{1,3,2,0:T(8,128)} fusion(f32[1,512,24,64]{1,3,2,0:T(8,128)S(1)} %bitcast.526, f32[512,24,64]{0,2,1:T(8,128)S(1)} %fusion.156, f32[512,24,64]{0,2,1:T(8,128)S(1)} %bitcast.527, f32[24,512]{1,0:T(8,128)S(1)} %copy-done.95, f32[24,512]{1,0:T(8,128)S(1)} %bitcast_add_fusion.12, f32[512,512]{1,0:T(8,128)S(1)} %copy-done.69, ...), kind=kOutput, calls=%fused_computation.95 | convolution fusion | flops 4866441216 | bytes 14041184 | tf_op jit(solution)/shard_map/ghts,gshp->gthp/dot_general | solution.py:114
  532.9 22.5 %fusion.233 = f32[24,512,512]{2,1,0:T(8,128)S(1)} fusion(f32[512,24,64]{0,2,1:T(8,128)} %bitcast.531, f32[512,24,64]{0,2,1:T(8,128)} %bitcast.528), kind=kOutput, calls=%fused_computation.370 | convolution fusion | flops 4831838208 | bytes 31457280 | tf_op jit(solution)/shard_map/gthp,gshp->ghts/dot_general | solution.py:152
  555.5 50.4 %fusion.14 = (f32[24,512]{1,0:T(8,128)}, f32[24,512]{1,0:T(8,128)}, f32[24,512]{1,0:T(8,128)}, f32[512,512]{1,0:T(8,128)}, f32[512,512]{1,0:T(8,128)}, /*index=5...) fusion(f32[24,512]{1,0:T(8,128)S(1)} %copy-done.93, f32[24,512]{1,0:T(8,128)S(1)} %copy-done.98, ...), kind=kOutput, calls=%fused_computation.16 | convolution fusion | flops 4982235136 | bytes 36405248 | tf_op jit(solution)/shard_map/gthp,gshp->ghts/dot_general | solution.py:152
  615.8 7.3 convolution_bitcast_fusion.2
  644.8 18.6 %fusion.18 = f32[24,1,64,128]{3,1,2,0:T(1,128)S(1)} fusion(f32[16,24,1,1]{0,2,3,1:T(1,128)S(1)} %copy.369, f32[16,24,64,128]{3,2,1,0:T(8,128)} %bitcast.556), kind=kOutput, calls=%fused_computation.20 | convolution fusion | flops 37748736 | bytes 13370880 | tf_op jit(solution)/shard_map/cgh,cghpn->ghpn/dot_general | solution.py:48
  669.5 128.1 %all-gather.19.cloned.1.call-done = f32[384,64,128]{2,1,0:T(8,128)} async-done(((f32[24,64,128]{2,1,0:T(8,128)}), f32[384,64,128]{2,1,0:T(8,128)}) %all-gather.19.cloned.1.call-update) | async-done | bytes 12582928 | tf_op jit(solution)/shard_map/all_gather | solution.py:166
  797.6 18.6 %fusion.20 = f32[24,1,64,128]{3,1,2,0:T(1,128)S(1)} fusion(f32[16,24,1,1]{0,2,3,1:T(1,128)S(1)} %copy.362, f32[16,24,64,128]{3,2,1,0:T(8,128)} %bitcast.557), kind=kOutput, calls=%fused_computation.22 | convolution fusion | flops 37748736 | bytes 13370880 | tf_op jit(solution)/shard_map/cgh,cghpn->ghpn/dot_general | solution.py:48
  856.6 26.5 %fusion.58 = f32[1,512,24,64]{1,3,2,0:T(8,128)} fusion(f32[512,24,64]{0,2,1:T(8,128)} %get-tuple-element.172, f32[1,512,24,64]{1,3,2,0:T(8,128)} %bitcast.533, f32[512,24,64]{0,2,1:T(8,128)} %bitcast.532, f32[24,512]{1,0:T(8,128)} %copy.308, f32[24,512]{1,0:T(8,128)} %copy-done.100, f32[512,512]{1,0:T(8,128)} %fusion.159, ...), kind=kOutput, calls=%fused_computation.91 | convolution fusion | flops 4866441216 | bytes 14041184 | tf_op jit(solution)/shard_map/ghts,gthp->gshp/dot_general | solution.py:153
  883.2 25.0 %fusion.59 = f32[1,512,24,64]{1,3,2,0:T(8,128)} fusion(f32[512,24,64]{0,2,1:T(8,128)S(1)} %copy-done.51, f32[1,512,24,64]{1,3,2,0:T(8,128)S(1)} %bitcast.549, f32[512,24,64]{0,2,1:T(8,128)S(1)} %bitcast.548, f32[24,512]{1,0:T(8,128)S(1)} %copy-done.94, f32[24,512]{1,0:T(8,128)S(1)} %copy-done.99, f32[512,512]{1,0:T(8,128)S(1)} %copy-done.68, ...), kind=kOutput, calls=%fused_computation.93 | convolution fusion | flops 4866441216 | bytes 14041184 | tf_op jit(solution)/shard_map/ghts,gthp->gshp/dot_general | solution.py:153
  922.8 9.7 fusion.222
  939.3 7.8 broadcast_multiply_fusion.6
  952.7 8.1 pad_add_fusion
  987.1 21.7 %reduce-scatter.3.cloned.1.call-done = f32[384,3352]{0,1:T(8,128)} async-done(((f32[768,3352]{0,1:T(8,128)}), f32[384,3352]{0,1:T(8,128)}) %reduce-scatter.3.cloned.1.call-update) | async-done | bytes 5148688 | tf_op jit(solution)/shard_map/reduce_scatter | solution.py:213
  1025.8 45.6 %all-reduce.10 = (f32[4,1792]{1,0:T(4,128)}, f32[1792]{0:T(1024)}, f32[768]{0:T(1024)}, f32[1536]{0:T(1024)}, f32[24]{0:T(128)}, /*index=5*/f32[24]{0:T(128)}, f32[24]{0:T(128)}) all-reduce(f32[4,1792]{1,0:T(4,128)S(1)} %maximum_add_fusion, f32[1792]{0:T(1024)S(1)} %add.415, ...), channel_id=1, replica_groups=mesh['dp'=2,'seq'=16] {'dp','seq'}, use_global_device_ids=true, to_apply=%region_44.45 | all-reduce | flops 11336 | bytes 90688 | tf_op jit(solution)/shard_map/psum | solution.py:217
  1075.3 181.9 %all-reduce.14.cloned.1.call-done = (f32[384,3352]{0,1:T(8,128)}, f32[768,768]{1,0:T(8,128)}) async-done(((f32[384,3352]{0,1:T(8,128)}, f32[768,768]{1,0:T(8,128)}), (f32[384,3352]{0,1:T(8,128)}, f32[768,768]{1,0:T(8,128)})) %all-reduce.14.cloned.1.call-update) | async-done | bytes 7507984 | tf_op jit(solution)/shard_map/psum | solution.py:216
  (511 shorter events, 354.9 us)
Async XLA Ops:
  7.2 20.0 %all-gather.11.cloned.1.call-start = ((), (), s32[]{:S(2)}) async-start(), calls=%async_computation.2 | async-start | bytes 7723008 | tf_op jit(solution)/shard_map/all_gather | solution.py:83
  8.0 106.8 %all-gather.13.cloned.1.call-start = ((), (), s32[]{:S(2)}) async-start(), calls=%async_computation.3 | async-start | bytes 3538944 | tf_op jit(solution)/shard_map/all_gather | solution.py:84
  8.7 238.6 %all-gather.15.cloned.1.call-start = ((), (), s32[]{:S(2)}) async-start(), calls=%async_computation.6 | async-start | bytes 13369344 | tf_op jit(solution)/shard_map/all_gather | solution.py:122
  9.9 44.5 %copy-start.126 = (f32[24]{0:T(128)}, f32[24]{0:T(128)S(1)}, u32[]{:S(2)}) copy-start(f32[24]{0:T(128)S(1)} %get-tuple-element.179) | copy-start | bytes 292
  43.2 24.0 %collective-permute-start.1 = (f32[1,3,1792]{2,0,1:T(1,128)}, f32[1,3,1792]{2,0,1:T(1,128)}, u32[]{:S(2)}, u32[]{:S(2)}) collective-permute-start(f32[1,3,1792]{2,0,1:T(1,128)} %copy.302), channel_id=1, source_target_pairs={{0,1},{1,2},{2,3},{3,4},{4,5},{5,6},{6,7},{7,8},{8,9},{9,10},{10,1... | collective-permute-start | bytes 64520 | tf_op jit(solution)/shard_map/ppermute | solution.py:23
  48.0 19.9 %collective-permute-start = (f32[1,3,1792]{2,0,1:T(1,128)}, f32[1,3,1792]{2,0,1:T(1,128)}, u32[]{:S(2)}, u32[]{:S(2)}) collective-permute-start(f32[1,3,1792]{2,0,1:T(1,128)} %copy.287), channel_id=1, source_target_pairs={{0,1},{1,2},{2,3},{3,4},{4,5},{5,6},{6,7},{7,8},{8,9},{9,10},{10,1... | collective-permute-start | bytes 64520 | tf_op jit(solution)/shard_map/ppermute | solution.py:23
  56.6 39.3 %copy-start.56 = (f32[1,512,24]{2,1,0:T(8,128)}, f32[1,512,24]{2,1,0:T(8,128)S(1)}, u32[]{:S(2)}) copy-start(f32[1,512,24]{2,1,0:T(8,128)S(1)} %get-tuple-element.168) | copy-start | bytes 147460
  95.6 305.3 %all-gather.17.cloned.1.call-start = ((), (), s32[]{:S(2)}) async-start(), calls=%async_computation.7 | async-start | bytes 13369344 | tf_op jit(solution)/shard_map/all_gather | solution.py:122
  112.7 532.0 %all-gather.21.cloned.1.call-start = ((), (), s32[]{:S(2)}) async-start(), calls=%async_computation.9 | async-start | bytes 13369344 | tf_op jit(solution)/shard_map/all_gather | solution.py:166
  114.7 88.6 %copy-start.66 = (f32[24,512]{0,1:T(8,128)S(1)}, f32[24,512]{0,1:T(8,128)}, u32[]{:S(2)}) copy-start(f32[24,512]{0,1:T(8,128)} %get-tuple-element.169) | copy-start | bytes 147460
  208.1 215.0 %copy-start.100 = (f32[24,512]{1,0:T(8,128)}, f32[24,512]{1,0:T(8,128)S(1)}, u32[]{:S(2)}) copy-start(f32[24,512]{1,0:T(8,128)S(1)} %bitcast_add_fusion.12) | copy-start | bytes 147460
  214.0 209.0 %copy-start.6 = (f32[1,512,1536]{1,2,0:T(8,128)}, f32[1,512,1536]{1,2,0:T(8,128)S(1)}, u32[]{:S(2)}) copy-start(f32[1,512,1536]{1,2,0:T(8,128)S(1)} %copy.304) | copy-start | bytes 9437188
  461.9 169.9 %copy-start.114 = (f32[512]{0:T(512)}, f32[512]{0:T(512)S(1)}, u32[]{:S(2)}) copy-start(f32[512]{0:T(512)S(1)} %get-tuple-element.163) | copy-start | bytes 6148
  465.0 163.9 %copy-start.116 = (f32[512]{0:T(512)}, f32[512]{0:T(512)S(1)}, u32[]{:S(2)}) copy-start(f32[512]{0:T(512)S(1)} %get-tuple-element.161) | copy-start | bytes 6148
  494.4 303.2 %all-gather.19.cloned.1.call-start = ((), (), s32[]{:S(2)}) async-start(), calls=%async_computation.8 | async-start | bytes 13369344 | tf_op jit(solution)/shard_map/all_gather | solution.py:166
  515.0 472.1 %reduce-scatter.5.cloned.1.call-start = ((), (), s32[]{:S(2)}) async-start(), calls=%async_computation.5 | async-start | bytes 7077888 | tf_op jit(solution)/shard_map/reduce_scatter | solution.py:214
  635.9 372.9 %reduce-scatter.3.cloned.1.call-start = ((), (), s32[]{:S(2)}) async-start(), calls=%async_computation.4 | async-start | bytes 15446016 | tf_op jit(solution)/shard_map/reduce_scatter | solution.py:213
  949.3 19.5 %collective-permute-start.2 = (f32[1,3,1792]{2,0,1:T(1,128)}, f32[1,3,1792]{2,0,1:T(1,128)}, u32[]{:S(2)}, u32[]{:S(2)}) collective-permute-start(f32[1,3,1792]{2,0,1:T(1,128)} %copy.326), channel_id=1, source_target_pairs={{1,0},{2,1},{3,2},{4,3},{5,4},{6,5},{7,6},{8,7},{9,8},{10,9},{11,1... | collective-permute-start | bytes 64520 | tf_op jit(solution)/shard_map/ppermute | solution.py:23
  950.6 19.1 %collective-permute-start.3 = (f32[1,3,1792]{2,0,1:T(1,128)}, f32[1,3,1792]{2,0,1:T(1,128)}, u32[]{:S(2)}, u32[]{:S(2)}) collective-permute-start(f32[1,3,1792]{2,0,1:T(1,128)} %copy.345), channel_id=1, source_target_pairs={{1,0},{2,1},{3,2},{4,3},{5,4},{6,5},{7,6},{8,7},{9,8},{10,9},{11,1... | collective-permute-start | bytes 64520 | tf_op jit(solution)/shard_map/ppermute | solution.py:23
  986.5 270.7 %all-reduce.14.cloned.1.call-start = ((), (), s32[]{:S(2)}) async-start(), calls=%async_computation.10 | async-start | bytes 15015936 | tf_op jit(solution)/shard_map/psum | solution.py:216
  1021.3 50.2 %copy-start.43 = (bf16[2,1,512,768]{3,2,1,0:T(8,128)(2,1)S(1)}, bf16[2,1,512,768]{3,2,1,0:T(8,128)(2,1)}, u32[]{:S(2)}) copy-start(bf16[2,1,512,768]{3,2,1,0:T(8,128)(2,1)} %param.15) | copy-start | bytes 4718596
  1021.3 50.2 %copy-start.48 = (bf16[2,1,512,768]{3,2,1,0:T(8,128)(2,1)S(1)}, bf16[2,1,512,768]{3,2,1,0:T(8,128)(2,1)}, u32[]{:S(2)}) copy-start(bf16[2,1,512,768]{3,2,1,0:T(8,128)(2,1)} %param.25) | copy-start | bytes 4718596
  1021.3 50.2 %copy-start.127 = (f32[512]{0:T(512)S(1)}, f32[512]{0:T(512)}, u32[]{:S(2)}) copy-start(f32[512]{0:T(512)} %get-tuple-element.158) | copy-start | bytes 6148
  1021.3 50.2 %copy-start.130 = (f32[512]{0:T(512)S(1)}, f32[512]{0:T(512)}, u32[]{:S(2)}) copy-start(f32[512]{0:T(512)} %get-tuple-element.177) | copy-start | bytes 6148
  (138 other events, 1185.3 us)
Sparse Core Ops, SparseCore 0:
  9.6 17.6 all-gather.10
  28.8 12.1 all-gather.12
  95.7 151.6 all-gather.14
  250.6 150.2 all-gather.16
  494.5 150.1 all-gather.20
  647.4 150.1 all-gather.18
  800.5 10.7 reduce-scatter.4
  986.7 22.1 reduce-scatter.2
  1016.4 240.7 all-reduce.13
where the time goes:
time: 1280 us; the launch traced here: 1270 us
  waiting for transfers between devices  476 us (37%)
  matrix products  391 us (31%)
  other arithmetic  133 us (10%)
  local copies, waits for them, and re-layouts  124 us (10%)
  blocking collectives  119 us (9%)
  between operations  15.9 us (1%)
    psum x1, waiting for transfers between devices, per_device(): share_in, share_out = lax.psum((rows_in, rows_out), 'seq')  182 us
    all_gather x2, waiting for transfers between devices, per_device(): lax.all_gather(d_start[None], 'seq', axis=0, tiled=True)  131 us
    all_gather x2, waiting for transfers between devices, per_device(): lax.all_gather(local_state[None], 'seq', axis=0, tiled=True)  123 us
    dot_general x4, matrix products, fold_states(): return jnp.einsum('cgh,cghpn->ghpn', weights, piece, precision=HIGH)  73.7 us
    all_gather x2, blocking collectives, per_device(): totals = lax.all_gather(block_total[None], 'seq', axis=0, tiled=True)  73.3 us
    dot_general x2, matrix products, per_device(): d_mixing = jnp.einsum('gthp,gshp->ghts', d_heads, x_heads, precision=HIGH)  72.9 us
    dot_general x2, matrix products, per_device(): y_inner = jnp.einsum('ghts,gshp->gthp', mixing, x_heads, precision=HIGH)  61.9 us
    dot_general x2, matrix products, per_device(): d_x = d_x + jnp.einsum('ghts,gthp->gshp', mixing, d_heads, precision=HIGH)  51.5 us
  transfers between devices with their start and end apart: 13, of which 7 were waited for; matrix products, arithmetic and copies ran while one was open for 42% of the time, Pallas kernels for 0%

commit v1 on v0

v1 whole, which is shorter than its diff:
```python
import functools

import jax
import jax.numpy as jnp
from jax import lax
from jax.experimental import pallas as pl
from jax.experimental.pallas import tpu as pltpu
from jax.sharding import PartitionSpec as P

D = 768
DIN = 1536
HEADS = 24
HEAD_DIM = 64
STATE = 128
CONV = 4
XBC = 1792
PROJ = 3352
EPS = 1e-05
LOG2E = 1.4426950408889634
CHUNK = 128
TILE = 256
HALO = 16
UNIT = 16
KIND = jnp.bfloat16
F32 = jnp.float32
BF16 = jnp.bfloat16
VMEM_LIMIT = 62 * 1024 * 1024


def mm(a, b):
    return lax.dot_general(a, b, (((1,), (0,)), ((), ())), preferred_element_type=F32)


def mm_nt(a, b):
    return lax.dot_general(a, b, (((1,), (1,)), ((), ())), preferred_element_type=F32)


def mm_tn(a, b):
    return lax.dot_general(a, b, (((0,), (0,)), ((), ())), preferred_element_type=F32)


def split2(v):
    hi = v.astype(BF16)
    return hi, (v - hi.astype(F32)).astype(BF16)


def split3(v):
    hi = v.astype(BF16)
    rest = v - hi.astype(F32)
    mid = rest.astype(BF16)
    return hi, mid, (rest - mid.astype(F32)).astype(BF16)


def iota(shape, dim):
    return lax.broadcasted_iota(jnp.int32, shape, dim)


def spread_matrix(start, width):
    head = iota((2 * STATE, width), 0) & (STATE - 1)
    column = (iota((2 * STATE, width), 1) + start) >> 6
    return jnp.where(head == column, 1.0, 0.0).astype(BF16)


def gather_matrix():
    return jnp.where((iota((DIN, STATE), 0) >> 6) == iota((DIN, STATE), 1), 1.0, 0.0).astype(BF16)


def spread(v, matrix):
    return mm(jnp.concatenate(split2(v), axis=1), matrix)


def head_sums(v, matrix, parts=3):
    pieces = split3(v) if parts == 3 else split2(v)
    total = mm(pieces[0], matrix)
    for piece in pieces[1:]:
        total = total + mm(piece, matrix)
    return total


def fine_nt(a, b):
    ah, al = split2(a)
    bh, bl = split2(b)
    return mm_nt(jnp.concatenate([ah, ah, al], axis=1), jnp.concatenate([bh, bl, bh], axis=1))


def halves(v):
    return jnp.concatenate(split2(v), axis=0)


def triangle(upper):
    row, column = iota((CHUNK, CHUNK), 0), iota((CHUNK, CHUNK), 1)
    keep = column >= row if upper else column <= row
    return jnp.where(keep, 1.0, 0.0).astype(BF16)


def tri_sum(tri, v):
    return mm(jnp.concatenate([tri] * 3, axis=1), jnp.concatenate(split3(v), axis=0))


def head_params(hp_ref):
    hp = hp_ref[...]
    decay = -jnp.exp(-4.0 + 0.25 * hp[0:1])
    bias = -9.0 + 0.25 * hp[1:2]
    return decay, bias, hp


def sigmoid(v):
    return 1.0 / (1.0 + jnp.exp(-v))


def norm_rows(tok, gain):
    src = tok.astype(F32)
    scale = lax.rsqrt(jnp.mean(src * src, axis=-1, keepdims=True) + EPS)
    return src, scale, (src * scale * gain).astype(BF16)


def pair_masks():
    low = iota((CHUNK, STATE), 1) < HEAD_DIM
    return low, jnp.logical_not(low)


def doubled(v):
    low, high = pair_masks()
    wide = v.astype(F32)
    return jnp.concatenate([jnp.where(low, wide, 0.0).astype(BF16), jnp.where(high, wide, 0.0).astype(BF16)], axis=0)


def k1_body(tok_ref, halo_ref, w_ref, ws_ref, cw_ref, cb_ref, ng_ref, hp_ref,
            gate_ref, cin_ref, cout_ref, bc_ref, ypart_ref, info_ref, sl_ref, sdev_ref, tot_ref,
            an, u, ub, dt2, tw2):
    T = tok_ref.shape[1]
    NC = T // CHUNK
    decay, bias, hp = head_params(hp_ref)
    decay2 = decay * LOG2E
    gain = ng_ref[...]
    first = lax.axis_index("seq") == 0
    an[0:HALO] = jnp.where(first, 0.0, norm_rows(halo_ref[0], gain)[2].astype(F32)).astype(BF16)
    an[HALO:] = norm_rows(tok_ref[0], gain)[2]
    arg = mm_nt(an[HALO:], ws_ref[...]) + bias
    dt = jnp.maximum(arg, 0.0) + jnp.log1p(jnp.exp(-jnp.abs(arg)))
    info_ref[0, 0] = arg
    info_ref[0, 1] = dt
    dt2[...] = jnp.concatenate(split2(dt), axis=1)
    tri = triangle(False)
    total = jnp.zeros((1, STATE), F32)
    for c in range(NC):
        rows = slice(c * CHUNK, (c + 1) * CHUNK)
        lc = tri_sum(tri, dt[rows] * decay2)
        info_ref[0, 2, rows] = lc
        total = total + lc[CHUNK - 1:CHUNK]
        tw2[rows] = jnp.concatenate(split2(jnp.exp2(lc[CHUNK - 1:CHUNK] - lc)), axis=1)

    tot_ref[pl.ds(pl.program_id(0), 1)] = total

    @pl.loop(0, DIN // TILE)
    def _(j):
        cols = pl.ds(pl.multiple_of(j * TILE, TILE), TILE)
        gate_ref[0, :, cols] = mm_nt(an[HALO:], w_ref[cols, :])

    def conv_tile(j, cols):
        wcols = pl.ds(pl.multiple_of(DIN + j * TILE, TILE), TILE)
        cin_ref[0, :, cols] = mm_nt(an[...], w_ref[wcols, :])
        out = cb_ref[:, cols]
        for k in range(CONV):
            out = out + cw_ref[k:k + 1, cols] * cin_ref[0, HALO - CONV + 1 + k:HALO - CONV + 1 + k + T, cols]
        cout_ref[0, :, cols] = out
        return out * sigmoid(out)

    @pl.loop(0, DIN // TILE)
    def _(j):
        cols = pl.ds(pl.multiple_of(j * TILE, TILE), TILE)
        x = conv_tile(j, cols)
        matrix = spread_matrix(j * TILE, TILE)
        ux = x * mm(dt2[...], matrix)
        u[:, cols] = ux.astype(BF16)
        hi, lo = split2(ux * mm(tw2[...], matrix))
        for c in range(NC):
            rows = slice(c * CHUNK, (c + 1) * CHUNK)
            ub[c, 0:CHUNK, cols] = hi[rows]
            ub[c, CHUNK:, cols] = lo[rows]
        skip_tile = spread(jnp.broadcast_to(hp[2:3], (8, STATE)), matrix)[0:1]
        ypart_ref[0, :, cols] = x * skip_tile

    bc_ref[0] = conv_tile(DIN // TILE, pl.ds(DIN, TILE))

    causal = iota((CHUNK, CHUNK), 0) >= iota((CHUNK, CHUNK), 1)
    sdev_ref[0] = jnp.zeros((STATE, DIN), F32)

    @pl.loop(0, NC)
    def _(c):
        rows = pl.ds(pl.multiple_of(c * CHUNK, CHUNK), CHUNK)
        b = bc_ref[0, rows, 0:STATE]
        gram = jnp.where(causal, fine_nt(bc_ref[0, rows, STATE:2 * STATE], b), 0.0)
        b16 = b.astype(BF16)
        lc = info_ref[0, 2, rows]
        lct = lc.T
        sl_ref[0, c] = sdev_ref[0]
        total = jnp.exp2(jnp.broadcast_to(lc[CHUNK - 1:CHUNK], (8, STATE)))
        keep = spread(total, spread_matrix(0, DIN))[0:1]
        sdev_ref[0] = keep * sdev_ref[0] + mm_tn(jnp.concatenate([b16, b16], axis=0), ub[c])
        for p in range(HEADS // 2):
            cols = slice(p * STATE, (p + 1) * STATE)
            mixes = []
            for h in (2 * p, 2 * p + 1):
                gap = lc[:, h:h + 1] - lct[h:h + 1, :]
                mixes.append((gram * jnp.exp2(jnp.minimum(gap, 0.0))).astype(BF16))
            ypart_ref[0, rows, cols] = ypart_ref[0, rows, cols] + mm(jnp.concatenate(mixes, axis=1), doubled(u[rows, cols]))

    sl_ref[0, NC] = sdev_ref[0]


def whole(shape):
    rank = len(shape)
    return pl.BlockSpec(shape, lambda m: (0,) * rank)


def per_micro(shape, buffers=None):
    rank = len(shape)
    mode = None if buffers is None else pl.Buffered(buffers)
    return pl.BlockSpec((1,) + shape, lambda m: (m,) + (0,) * rank, pipeline_mode=mode)


def call(body, grid, ins, outs, scratch, name):
    return pl.pallas_call(
        body,
        grid=grid,
        in_specs=[s for s, _ in ins],
        out_specs=[s for s, _ in outs],
        out_shape=[o for _, o in outs],
        scratch_shapes=scratch,
        compiler_params=pltpu.CompilerParams(vmem_limit_bytes=VMEM_LIMIT, dimension_semantics=("arbitrary",) * len(grid)),
        name=name,
    )(*[a for _, a in ins])


def k1(tok, halo, w, ws, cw, cb, ng, hp):
    M, T, _ = tok.shape
    NC = T // CHUNK
    S = lambda shape, dt: (per_micro(shape), jax.ShapeDtypeStruct((M,) + shape, dt))
    return call(
        k1_body, (M,),
        [(per_micro((T, D)), tok), (per_micro((HALO, D)), halo), (whole(w.shape), w), (whole(ws.shape), ws),
         (whole(cw.shape), cw), (whole(cb.shape), cb), (whole(ng.shape), ng), (whole(hp.shape), hp)],
        [S((T, DIN), F32), S((HALO + T, XBC), F32), S((T, XBC), F32), S((T, 2 * STATE), F32), S((T, DIN), F32),
         S((3, T, STATE), F32), S((NC + 1, STATE, DIN), F32), S((STATE, DIN), F32),
         (whole((M, STATE)), jax.ShapeDtypeStruct((M, STATE), F32))],
        [pltpu.VMEM((HALO + T, D), BF16), pltpu.VMEM((T, DIN), BF16), pltpu.VMEM((NC, 2 * CHUNK, DIN), BF16),
         pltpu.VMEM((T, 2 * STATE), BF16), pltpu.VMEM((T, 2 * STATE), BF16)],
        "forward_local",
    )


def chunk_totals(info_ref, NC):
    return [info_ref[0, 2, (c + 1) * CHUNK - 1:(c + 1) * CHUNK] for c in range(NC)]


def product_sum(left, right, cols):
    total = mm(left[0], right[0, :, cols])
    for m in range(1, left.shape[0]):
        total = total + mm(left[m], right[m, :, cols])
    return total


def put_tile(gtile_ref, d, tile, part):
    count = part.shape[0] // UNIT
    gtile_ref[d, pl.ds(tile * count, count)] = part.reshape(count, UNIT, STATE)


def clear_tiles(gtile_ref, rows, tiles):
    low, high = tiles * (rows // UNIT), gtile_ref.shape[1]
    if high > low:
        gtile_ref[:, low:] = jnp.zeros((gtile_ref.shape[0], high - low, UNIT, STATE), BF16)


def weight_tiles(gtile_ref, rows, left, right, count):
    @pl.loop(0, count)
    def _(j):
        part = product_sum(left, right, pl.ds(pl.multiple_of(j * STATE, STATE), STATE)).astype(BF16)
        for d in range(gtile_ref.shape[0]):
            put_tile(gtile_ref, d, j, part[d * rows:(d + 1) * rows])


def k2_body(tok_ref, cot_ref, ng_ref, og_ref, wo_ref, hp_ref, gate_ref, ypart_ref, bc_ref, info_ref, sl_ref, start_ref,
            mixed_ref, dgate_ref, dy_ref, r_ref, gl_ref, gdev_ref, ogr_ref, gtile_ref,
            y, dbr, branch, branch_t, norm_t, oscale, cot_all):
    m = pl.program_id(0)
    T = tok_ref.shape[1]
    NC = T // CHUNK
    matrix = spread_matrix(0, DIN)
    gather = gather_matrix()
    src, _, normed = norm_rows(tok_ref[0], ng_ref[...])
    norm_t[m] = normed.T
    cot_all[m] = cot_ref[0]

    @pl.when(m == 0)
    def _():
        ogr_ref[...] = jnp.zeros_like(ogr_ref)

    totals = chunk_totals(info_ref, NC)
    before = jnp.zeros((1, STATE), F32)
    for c in range(NC):
        rows = slice(c * CHUNK, (c + 1) * CHUNK)
        keep = spread(jnp.exp2(jnp.broadcast_to(before, (8, STATE))), matrix)[0:1]
        before = before + totals[c]
        state = halves(sl_ref[0, c].astype(F32) + keep * start_ref[0].astype(F32))
        c16 = bc_ref[0, rows, STATE:2 * STATE].astype(BF16)
        lift = spread(jnp.exp2(info_ref[0, 2, rows]), matrix)
        yc = ypart_ref[0, rows] + lift * mm(jnp.concatenate([c16, c16], axis=1), state)
        y[rows] = yc
        g = gate_ref[0, rows]
        gated = yc * (g * sigmoid(g))
        scale = lax.rsqrt(jnp.mean(gated * gated, axis=-1, keepdims=True) + EPS)
        oscale[rows] = jnp.broadcast_to(scale, (CHUNK, STATE))
        branch[rows] = (gated * scale * og_ref[...]).astype(BF16)
    branch_t[m] = branch[...].T
    cot = cot_ref[0]
    for j in range(D // TILE):
        cols = slice(j * TILE, (j + 1) * TILE)
        mixed_ref[0, :, cols] = (tok_ref[0, :, cols].astype(F32) + mm(branch[...], wo_ref[:, cols])).astype(BF16)

    @pl.loop(0, DIN // TILE)
    def _(j):
        cols = pl.ds(pl.multiple_of(j * TILE, TILE), TILE)
        dbr[:, cols] = mm_nt(cot, wo_ref[cols, :])

    gdev_ref[0] = jnp.zeros((STATE, DIN), F32)

    @pl.loop(0, NC)
    def _(i):
        c = NC - 1 - i
        rows = pl.ds(pl.multiple_of(c * CHUNK, CHUNK), CHUNK)
        g = gate_ref[0, rows]
        yc = y[rows]
        db = dbr[rows]
        scale = oscale[rows][:, 0:1]
        sig = sigmoid(g)
        act = g * sig
        gated = yc * act
        unit = gated * scale
        ogr_ref[...] += jnp.sum(db * unit, axis=0, keepdims=True)
        e = db * og_ref[...]
        mean = jnp.mean(e * unit, axis=-1, keepdims=True)
        dgated = scale * (e - unit * mean)
        dgate_ref[m, rows] = (dgated * yc * (sig * (1.0 + g * (1.0 - sig)))).astype(BF16)
        dy = (dgated * act).astype(BF16)
        dy_ref[0, rows] = dy
        dyf = dy.astype(F32)
        r_ref[0, rows] = head_sums(dyf * yc, gather)
        lc = info_ref[0, 2, rows]
        lifted = halves(dyf * spread(jnp.exp2(lc), matrix))
        c16 = bc_ref[0, rows, STATE:2 * STATE].astype(BF16)
        gl_ref[0, c] = gdev_ref[0]
        total = jnp.exp2(jnp.broadcast_to(lc[CHUNK - 1:CHUNK], (8, STATE)))
        keep = spread(total, matrix)[0:1]
        gdev_ref[0] = keep * gdev_ref[0] + mm_tn(jnp.concatenate([c16, c16], axis=0), lifted)

    @pl.when(m == pl.num_programs(0) - 1)
    def _():
        dp = gtile_ref.shape[0]
        rows = D // dp
        weight_tiles(gtile_ref, rows, norm_t, dgate_ref, DIN // STATE)
        clear_tiles(gtile_ref, rows, 24)

        @pl.loop(0, D // STATE)
        def _(j):
            part = product_sum(branch_t, cot_all, pl.ds(pl.multiple_of(j * STATE, STATE), STATE)).astype(BF16)
            for d in range(dp):
                for half in range(2):
                    low = (2 * d + half) * rows
                    put_tile(gtile_ref, d, 12 + half * 6 + j, part[low:low + rows])


def k2(tok, cot, ng, og, wo, hp, gate, ypart, bc, info, sl, start, dp, units):
    M, T, _ = tok.shape
    NC = T // CHUNK
    S = lambda shape, dt: (per_micro(shape), jax.ShapeDtypeStruct((M,) + shape, dt))
    W = lambda shape, dt: (whole(shape), jax.ShapeDtypeStruct(shape, dt))
    one = lambda a, n=1: (per_micro(a.shape[1:], n), a)
    all_ = lambda a: (whole(a.shape), a)
    return call(
        k2_body, (M,),
        [one(tok), one(cot), all_(ng), all_(og), all_(wo), all_(hp), one(gate), one(ypart, 1), one(bc), one(info), one(sl), one(start, 1)],
        [S((T, D), BF16), W((M, T, DIN), BF16), S((T, DIN), BF16), S((T, STATE), F32), S((NC, STATE, DIN), F32),
         S((STATE, DIN), F32), W((1, DIN), F32), W((dp, units, UNIT, STATE), BF16)],
        [pltpu.VMEM((T, DIN), F32), pltpu.VMEM((T, DIN), F32), pltpu.VMEM((T, DIN), BF16), pltpu.VMEM((M, DIN, T), BF16),
         pltpu.VMEM((M, D, T), BF16), pltpu.VMEM((T, STATE), F32), pltpu.VMEM((M, T, D), BF16)],
        "gate_and_out",
    )


def k3_body(hp_ref, cw_ref, cin_ref, cout_ref, bc_ref, info_ref, sl_ref, start_ref, dy_ref, r_ref, gl_ref, later_ref,
            dcin_ref, tail_ref, head_ref, dstep_ref, gcw_ref, gcb_ref, gskip_ref, ghead_ref,
            dconv, w, xdu, ub, dyl, dgt, dt_x, tail_x, bg):
    m = pl.program_id(0)
    T = cout_ref.shape[1]
    NC = T // CHUNK
    decay, _, hp = head_params(hp_ref)
    matrix = spread_matrix(0, DIN)
    gather = gather_matrix()
    skip = spread(jnp.broadcast_to(hp[2:3], (8, STATE)), matrix)[0:1]

    @pl.when(m == 0)
    def _():
        gcw_ref[...] = jnp.zeros_like(gcw_ref)
        gcb_ref[...] = jnp.zeros_like(gcb_ref)
        gskip_ref[...] = jnp.zeros_like(gskip_ref)
        ghead_ref[...] = jnp.zeros_like(ghead_ref)

    dconv[T:] = jnp.zeros((HALO, XBC), F32)
    tri_up = triangle(True)
    keeps_st = iota((CHUNK, CHUNK), 0) <= iota((CHUNK, CHUNK), 1)
    totals = chunk_totals(info_ref, NC)
    afters, befores = [jnp.zeros((1, STATE), F32)], [jnp.zeros((1, STATE), F32)]
    for c in range(NC):
        befores.append(befores[-1] + totals[c])
        afters.append(afters[-1] + totals[NC - 1 - c])
    afters = afters[::-1]

    for c in range(NC):
        rows = slice(c * CHUNK, (c + 1) * CHUNK)
        b = bc_ref[0, rows, 0:STATE]
        cc = bc_ref[0, rows, STATE:2 * STATE]
        gram_t = jnp.where(keeps_st, fine_nt(b, cc), 0.0)
        b, cc = b.astype(BF16), cc.astype(BF16)
        lc = info_ref[0, 2, rows]
        lct = lc.T
        dt = info_ref[0, 1, rows]
        dt_x[...] = spread(dt, matrix)
        tail_x[...] = spread(jnp.exp2(lc[CHUNK - 1:CHUNK] - lc), matrix)
        lift = spread(jnp.exp2(lc), matrix)
        dyl[...] = (dy_ref[0, rows].astype(F32) * lift).astype(BF16)
        wide8 = lambda v: spread(jnp.exp2(jnp.broadcast_to(v, (8, STATE))), matrix)[0:1]
        gc = gl_ref[0, c].astype(F32) + wide8(afters[c + 1]) * later_ref[0].astype(F32)
        gcb16 = gc.astype(BF16)
        s_in = sl_ref[0, c].astype(F32) + wide8(befores[c]) * start_ref[0].astype(F32)
        s_out_start = wide8(befores[c + 1]) * start_ref[0].astype(F32)
        if c + 1 < NC:
            s_out = sl_ref[0, c + 1].astype(F32) + s_out_start
        else:
            s_out = sl_ref[0, NC].astype(F32) + s_out_start
        bnd = head_sums(jnp.broadcast_to(jnp.sum(gc * s_out, axis=0, keepdims=True), (8, DIN)), gather)[0:1]
        bg[...] = mm(jnp.concatenate([b, b], axis=1), halves(gc))
        dgt[...] = jnp.zeros((CHUNK, CHUNK), F32)
        for p in range(HEADS // 2):
            cols = slice(p * STATE, (p + 1) * STATE)
            v = cout_ref[0, rows, cols]
            sig = sigmoid(v)
            x = v * sig
            dtx, tlx = dt_x[:, cols], tail_x[:, cols]
            ux = x * dtx
            u16 = ux.astype(BF16)
            ub[:, cols] = (ux * tlx).astype(BF16)
            dy = dy_ref[0, rows, cols]
            dyf = dy.astype(F32)
            dy2 = doubled(dy)
            decays, mixes = [], []
            for h in (2 * p, 2 * p + 1):
                gap = lct[h:h + 1, :] - lc[:, h:h + 1]
                e = jnp.exp2(jnp.minimum(gap, 0.0))
                decays.append(e)
                mixes.append((gram_t * e).astype(BF16))
            du = mm(jnp.concatenate(mixes, axis=1), dy2)
            dmix = mm_nt(u16, dy2)
            dgt[...] = dgt[...] + (dmix[:, :CHUNK] * decays[0] + dmix[:, CHUNK:] * decays[1])
            du_state = tlx * bg[:, cols]
            sk = skip[:, cols]
            dyx = dyf * x
            gskip_ref[:, cols] = gskip_ref[:, cols] + jnp.sum(dyx, axis=0, keepdims=True)
            w[:, cols] = dyx * sk + u16.astype(F32) * du + ux * du_state
            du = du + du_state
            xdu[:, cols] = x * du
            dx = dtx * du + sk * dyf
            dconv[rows, cols] = dx * (sig * (1.0 + v * (1.0 - sig)))
        dg16 = jnp.where(keeps_st, dgt[...], 0.0).astype(BF16)
        db = mm(dg16, cc) + mm_nt(ub[...], gcb16)
        dc = mm_tn(dg16, b) + mm_nt(dyl[...], s_in.astype(BF16))
        v = cout_ref[0, rows, DIN:XBC]
        sig = sigmoid(v)
        dconv[rows, DIN:XBC] = jnp.concatenate([db, dc], axis=1) * (sig * (1.0 + v * (1.0 - sig)))
        dl = r_ref[0, rows] - head_sums(w[...], gather)
        da = bnd + tri_sum(tri_up, dl)
        d_dt = head_sums(xdu[...], gather, 2) + da * decay
        arg = info_ref[0, 0, rows]
        dstep = d_dt * sigmoid(arg)
        dstep_ref[0, rows] = dstep.astype(BF16)
        ghead_ref[0:1] = ghead_ref[0:1] + decay * jnp.sum(da * dt, axis=0, keepdims=True)
        ghead_ref[1:2] = ghead_ref[1:2] + jnp.sum(dstep, axis=0, keepdims=True)

    head_ref[0] = dconv[0:8]

    @pl.loop(0, XBC // TILE)
    def _(j):
        cols = pl.ds(pl.multiple_of(j * TILE, TILE), TILE)
        own = dconv[0:T, cols]
        gcb_ref[:, cols] = gcb_ref[:, cols] + jnp.sum(own, axis=0, keepdims=True)
        total = None
        for k in range(CONV):
            low = HALO - CONV + 1 + k
            gcw_ref[k:k + 1, cols] = gcw_ref[k:k + 1, cols] + jnp.sum(own * cin_ref[0, low:low + T, cols], axis=0, keepdims=True)
            term = cw_ref[k:k + 1, cols] * dconv[CONV - 1 - k:CONV - 1 - k + T, cols]
            total = term if total is None else total + term
        dcin_ref[0, :, cols] = total.astype(BF16)
        tail_ref[0, :, cols] = total[T - HALO:]


def k3(hp, cw, cin, cout, bc, info, sl, start, dy, r, gl, later):
    M, T, _ = cout.shape
    S = lambda shape, dt: (per_micro(shape), jax.ShapeDtypeStruct((M,) + shape, dt))
    W = lambda shape, dt: (whole(shape), jax.ShapeDtypeStruct(shape, dt))
    one = lambda a: (per_micro(a.shape[1:]), a)
    all_ = lambda a: (whole(a.shape), a)
    V = pltpu.VMEM
    return call(
        k3_body, (M,),
        [all_(hp), all_(cw), one(cin), one(cout), one(bc), one(info), one(sl), one(start), one(dy), one(r), one(gl), one(later)],
        [S((T, XBC), BF16), S((HALO, XBC), F32), S((8, XBC), F32), S((T, STATE), BF16), W((CONV, XBC), F32), W((1, XBC), F32),
         W((1, DIN), F32), W((2, STATE), F32)],
        [V((T + HALO, XBC), F32), V((CHUNK, DIN), F32), V((CHUNK, DIN), F32), V((CHUNK, DIN), BF16), V((CHUNK, DIN), BF16),
         V((CHUNK, CHUNK), F32), V((CHUNK, DIN), F32), V((CHUNK, DIN), F32), V((CHUNK, DIN), F32)],
        "scan_backward",
    )


def k4_body(tok_ref, cot_ref, ng_ref, w_ref, ws_ref, cw_ref, dgate_ref, dcin_ref, dstep_ref, tail_ref, next_ref,
            gtok_ref, ngr_ref, gtile_ref,
            dc, dn, norm_t):
    m = pl.program_id(0)
    T = tok_ref.shape[1]

    @pl.when(m == 0)
    def _():
        ngr_ref[...] = jnp.zeros_like(ngr_ref)

    src, scale, normed = norm_rows(tok_ref[0], ng_ref[...])
    norm_t[m] = normed.T
    dc[m, 0:T, 0:XBC] = dcin_ref[0]
    dc[m, :, XBC:] = dstep_ref[0]
    nxt = next_ref[0]
    row = iota((HALO, XBC), 0)
    tail = tail_ref[0]
    for s in range(CONV - 1):
        extra = jnp.zeros((1, XBC), F32)
        for k in range(s + 1):
            extra = extra + cw_ref[k:k + 1] * nxt[s - k:s - k + 1]
        tail = tail + jnp.where(row == HALO - CONV + 1 + s, extra, 0.0)
    dc[m, T - HALO:T, 0:XBC] = tail.astype(BF16)

    for i in range(D // TILE):
        cols = slice(i * TILE, (i + 1) * TILE)
        dn[:, cols] = (mm(dgate_ref[0], w_ref[0:DIN, cols]) + mm(dc[m, :, 0:XBC], w_ref[DIN:DIN + XBC, cols])
                       + mm(dstep_ref[0], ws_ref[:, cols]))
    d_normed = dn[...]
    unit = src * scale
    ngr_ref[...] += jnp.sum(d_normed * unit, axis=0, keepdims=True)
    f = d_normed * ng_ref[...]
    mean = jnp.mean(f * unit, axis=-1, keepdims=True)
    gtok_ref[0] = (cot_ref[0].astype(F32) + scale * (f - unit * mean)).astype(BF16)

    @pl.when(m == pl.num_programs(0) - 1)
    def _():
        rows = D // gtile_ref.shape[0]
        weight_tiles(gtile_ref, rows, norm_t, dc, 15)
        clear_tiles(gtile_ref, rows, 15)


def k4(tok, cot, ng, w, ws, cw, dgate, dcin, dstep, tail, nxt, dp, units):
    M, T, _ = tok.shape
    S = lambda shape, dt: (per_micro(shape), jax.ShapeDtypeStruct((M,) + shape, dt))
    W = lambda shape, dt: (whole(shape), jax.ShapeDtypeStruct(shape, dt))
    one = lambda a: (per_micro(a.shape[1:]), a)
    all_ = lambda a: (whole(a.shape), a)
    V = pltpu.VMEM
    return call(
        k4_body, (M,),
        [one(tok), one(cot), all_(ng), all_(w), all_(ws), all_(cw), one(dgate), one(dcin), one(dstep), one(tail), one(nxt)],
        [S((T, D), BF16), W((1, D), F32), W((dp, units, UNIT, STATE), BF16)],
        [V((M, T, XBC + STATE), BF16), V((T, D), F32), V((M, D, T), BF16)],
        "projection_backward",
    )


MESH = pl.DeviceIdType.MESH
PLANE = 4
QUARTER = DIN // PLANE
DMA = pltpu.SemaphoreType.DMA


def places():
    seq = lax.axis_index("seq")
    return lax.axis_index("dp"), seq, lax.rem(seq, PLANE), lax.div(seq, PLANE)


def greet(devices):
    barrier = pltpu.get_barrier_semaphore()
    for device in devices:
        pl.semaphore_signal(barrier, inc=1, device_id=device, device_id_type=MESH)
    pl.semaphore_wait(barrier, len(devices))


def remote(src, dst, send, recv, device):
    return pltpu.make_async_remote_copy(
        src_ref=src, dst_ref=dst, send_sem=send, recv_sem=recv, device_id=device, device_id_type=MESH)


def open_body(ndp, nseq, win_ref, ws_ref, wout_ref, tok_ref, w_ref, wsall_ref, wo_ref, halo_ref, send, recv, hsend, hrecv):
    dp, seq, _, _ = places()
    nxt, prev = lax.rem(seq + 1, nseq), lax.rem(seq + nseq - 1, nseq)
    others = [lax.rem(dp + d, ndp) for d in range(1, ndp)]
    greet([(o, seq) for o in others] + [(dp, nxt), (dp, prev)])
    T = tok_ref.shape[1]
    width, rows = win_ref.shape[1], wout_ref.shape[0]
    columns = pl.ds(pl.multiple_of(dp * width, width), width)
    own_rows = pl.ds(pl.multiple_of(dp * rows, rows), rows)
    moves = [(ws_ref, wsall_ref.at[:, columns]), (win_ref.at[0:DIN + XBC], w_ref.at[:, columns]), (wout_ref, wo_ref.at[own_rows])]
    copies = [remote(tok_ref.at[:, T - HALO:T], halo_ref, hsend, hrecv, (dp, nxt))]
    for i, o in enumerate(others):
        for k, (src, dst) in enumerate(moves):
            copies.append(remote(src, dst, send.at[i, k], recv.at[i, k], (o, seq)))
    for copy in copies:
        copy.start()
    w_ref[:, columns] = win_ref[0:DIN + XBC]
    wsall_ref[:, columns] = ws_ref[...]
    wo_ref[own_rows] = wout_ref[...]
    for copy in copies:
        copy.wait()


def open_kernel(ndp, nseq, win, ws, wout, tok):
    vmem = pl.BlockSpec(memory_space=pltpu.VMEM)
    M = tok.shape[0]
    shape = lambda *s: jax.ShapeDtypeStruct(s, BF16)
    return pl.pallas_call(
        functools.partial(open_body, ndp, nseq),
        in_specs=[vmem] * 3 + [pl.BlockSpec(memory_space=pl.ANY)],
        out_specs=[vmem] * 4,
        out_shape=[shape(DIN + XBC, D), shape(STATE, D), shape(DIN, D), shape(M, HALO, D)],
        scratch_shapes=[DMA((ndp - 1, 3)), DMA((ndp - 1, 3)), DMA, DMA],
        compiler_params=pltpu.CompilerParams(collective_id=1, has_side_effects=True, vmem_limit_bytes=VMEM_LIMIT),
        name="gather_weights",
    )(win, ws, wout, tok)


def states_body(nseq, upward, s_ref, tot_ref, out_ref, stage, got, tots, pre, back, hop, sems, rsems, tsem, trsem, zs, zr, bs, br):
    dp, seq, p, z = places()
    M = s_ref.shape[0]
    Z = nseq // PLANE
    base = z * PLANE
    peers = [lax.rem(p + d, PLANE) for d in range(PLANE)]
    zup, zdown = lax.rem(seq + PLANE, nseq), lax.rem(seq + nseq - PLANE, nseq)
    greet([(dp, base + peers[d]) for d in range(1, PLANE)] + [(dp, zup), (dp, zdown)])
    columns = lambda q: pl.ds(pl.multiple_of(q * QUARTER, QUARTER), QUARTER)
    tots[0] = tot_ref[...]
    tcopies = [remote(tot_ref, tots.at[d], tsem.at[d - 1], trsem.at[d - 1], (dp, base + peers[d])) for d in range(1, PLANE)]
    for copy in tcopies:
        copy.start()
    first = []
    for m in range(M):
        stage[m] = s_ref[m].astype(stage.dtype)
        row = []
        for d in range(1, PLANE):
            copy = remote(stage.at[m, :, columns(peers[d])], got.at[m, d], sems.at[m, d - 1], rsems.at[m, d - 1], (dp, base + peers[d]))
            copy.start()
            row.append(copy)
        first.append(row)
    for copy in tcopies:
        copy.wait()
    shift = peers[0] * QUARTER
    order = list(range(PLANE))[::-1] if upward else list(range(PLANE))
    towards = zdown if upward else zup
    head = (z == Z - 1) if upward else (z == 0)
    tail = (z == 0) if upward else (z == Z - 1)
    last = []
    for m in range(M):
        for copy in first[m]:
            copy.wait_recv()
        matrix = spread_matrix(shift, QUARTER)
        slots = [lax.rem(p - q + PLANE, PLANE) for q in order]
        keep = [spread(jnp.exp2(jnp.broadcast_to(tots[s, m:m + 1], (8, STATE))), matrix)[0:1] for s in slots]

        got[m, 0] = s_ref[m, :, columns(p)].astype(got.dtype)
        link = remote(hop.at[m], pre.at[m], zs.at[m], zr.at[m], (dp, towards))

        @pl.when(head)
        def _():
            pre[m] = jnp.zeros_like(pre[m])

        @pl.when(jnp.logical_not(head))
        def _():
            link.wait_recv()

        run = pre[m].astype(F32)
        for i, q in enumerate(order):
            back[m, slots[i]] = run.astype(back.dtype)
            run = keep[i] * run + got[m, slots[i]].astype(F32)
        hop[m] = run.astype(hop.dtype)

        @pl.when(jnp.logical_not(tail))
        def _():
            link.start()

        for d in range(1, PLANE):
            to = lax.rem(p + PLANE - d, PLANE)
            copy = remote(back.at[m, d], out_ref.at[m, :, columns(p)], bs.at[m, d - 1], br.at[m, d - 1], (dp, base + to))
            copy.start()
            last.append(copy)
        out_ref[m, :, columns(p)] = back[m, 0]
    for row in first:
        for copy in row:
            copy.wait_send()
    for copy in last:
        copy.wait()
    for m in range(M):
        link = remote(hop.at[m], pre.at[m], zs.at[m], zr.at[m], (dp, towards))

        @pl.when(jnp.logical_not(tail))
        def _():
            link.wait_send()


def exchange(nseq, upward, s, tot, kind):
    M = s.shape[0]
    V = pltpu.VMEM
    vmem = pl.BlockSpec(memory_space=pltpu.VMEM)
    quarter = (STATE, QUARTER)
    return pl.pallas_call(
        functools.partial(states_body, nseq, upward),
        in_specs=[vmem] * 2,
        out_specs=vmem,
        out_shape=jax.ShapeDtypeStruct(s.shape, kind),
        scratch_shapes=[V(s.shape, kind), V((M, PLANE) + quarter, kind), V((PLANE,) + tot.shape, F32), V((M,) + quarter, kind),
                        V((M, PLANE) + quarter, kind), V((M,) + quarter, kind),
                        DMA((M, 3)), DMA((M, 3)), DMA((3,)), DMA((3,)), DMA((M,)), DMA((M,)), DMA((M, 3)), DMA((M, 3))],
        compiler_params=pltpu.CompilerParams(collective_id=3 if upward else 2, has_side_effects=True, vmem_limit_bytes=VMEM_LIMIT),
        name="states_later" if upward else "states_earlier",
    )(s, tot)


SMALL = (("cw", CONV, XBC), ("cb", 1, XBC), ("ng", 1, D), ("og", 1, DIN), ("skip", 1, DIN), ("head", 2, STATE))
SMALL_ROWS = 104


def small_pieces():
    row, found = 0, []
    for index, (_, rows, width) in enumerate(SMALL):
        for r in range(rows):
            for j in range(width // STATE):
                found.append((index, r, j, row))
                row += 1
    return found


def strided(count, step, body):
    @pl.loop(0, count // step)
    def _(i):
        body(pl.multiple_of(i * step, step))


def chunk_of(count):
    return max(c for c in range(1, 13) if count % c == 0)


def reduce_body(ndp, nseq, counts, *refs):
    nb = len(counts)
    ins, smalls, out_refs, small_out = refs[:nb], refs[nb:nb + 6], refs[nb + 6:2 * nb + 6], refs[2 * nb + 6]
    (r0, w1, st1, r1, w2, st2, r2, st3, r3, sm, smr, smy, smx, smz,
     s0s, s0r, s1s, s1r, s2s, s2r, s3s, s3r, t3s, t3r, t2s, t2r, t1s, t1r, ms, mr) = refs[2 * nb + 7:]
    dp, seq, p, z = places()
    Z = nseq // PLANE
    x, y = lax.rem(p, 2), lax.div(p, 2)
    others = [lax.rem(dp + d, ndp) for d in range(1, ndp)]
    px, py = seq + 1 - 2 * x, seq + 2 - 4 * y
    pz = [(lax.rem(z + d, Z) * PLANE + p) for d in range(1, Z)]
    greet([(o, seq) for o in others] + [(dp, px), (dp, py)] + [(dp, q) for q in pz])
    groups = []
    for b, count in enumerate(counts):
        half = count // 2
        groups += [(b, 0, half, (x, px), (y, py)), (b, half, half, (y, py), (x, px))]
    G = len(groups)
    n = [g[2] for g in groups]
    base = [sum(n[:g]) for g in range(G)]

    def begin0(g):
        b, start, size, _, _ = groups[g]
        copies = []
        for i, o in enumerate(others):
            copies.append(remote(ins[b].at[o, pl.ds(start, size)], r0.at[i, pl.ds(base[g], size)], s0s.at[g, i], s0r.at[g, i], (o, seq)))
        for copy in copies:
            copy.start()
        return copies

    def after0(g):
        b, start, size, (bit, peer), _ = groups[g]
        h = size // 2
        o1 = base[g] // 2
        c = chunk_of(h)

        def total(i):
            v = ins[b][dp, pl.ds(start + i, c)].astype(F32)
            for k in range(ndp - 1):
                v = v + r0[k, pl.ds(base[g] + i, c)].astype(F32)
            return v

        def body(i):
            w1[pl.ds(o1 + i, c)] = total(bit * h + i)
            st1[pl.ds(o1 + i, c)] = total((1 - bit) * h + i).astype(BF16)
        strided(h, c, body)
        copy = remote(st1.at[pl.ds(o1, h)], r1.at[pl.ds(o1, h)], s1s.at[g], s1r.at[g], (dp, peer))
        copy.start()
        return [copy]

    def after1(g):
        _, _, size, _, (bit, peer) = groups[g]
        q = size // 4
        o1, o2 = base[g] // 2, base[g] // 4
        c = chunk_of(q)

        def body(i):
            keep, give = o1 + bit * q + i, o1 + (1 - bit) * q + i
            w2[pl.ds(o2 + i, c)] = w1[pl.ds(keep, c)] + r1[pl.ds(keep, c)].astype(F32)
            st2[pl.ds(o2 + i, c)] = (w1[pl.ds(give, c)] + r1[pl.ds(give, c)].astype(F32)).astype(BF16)
        strided(q, c, body)
        copy = remote(st2.at[pl.ds(o2, q)], r2.at[pl.ds(o2, q)], s2s.at[g], s2r.at[g], (dp, peer))
        copy.start()
        return [copy]

    def after2(g):
        size = groups[g][2]
        q = size // 4
        e = q // Z
        o2 = base[g] // 4
        c = chunk_of(q)

        def body(i):
            v = w2[pl.ds(o2 + i, c)] + r2[pl.ds(o2 + i, c)].astype(F32)
            w2[pl.ds(o2 + i, c)] = v
            st3[pl.ds(o2 + i, c)] = v.astype(BF16)
        strided(q, c, body)
        copies = []
        for d in range(1, Z):
            to = lax.rem(z + d, Z)
            copies.append(remote(st3.at[pl.ds(o2 + to * e, e)], r3.at[d - 1, pl.ds(o2 // Z, e)], s3s.at[g, d - 1], s3r.at[g, d - 1], (dp, pz[d - 1])))
        for copy in copies:
            copy.start()
        return copies

    def where_out(g):
        b, start, size, (b1, _), (b2, _) = groups[g]
        h, q = size // 2, size // 4
        e = q // Z
        out = out_refs[b]
        return out, start + b1 * h, start + b1 * h + b2 * q, start + b1 * h + b2 * q + z * e, h, q, e

    def after3(g):
        out, _, _, at, _, q, e = where_out(g)
        o2 = base[g] // 4
        v = w2[pl.ds(o2 + z * e, e)]
        for d in range(Z - 1):
            v = v + r3[d, pl.ds(o2 // Z, e)].astype(F32)
        out[pl.ds(at, e)] = v.astype(BF16)
        copies = [remote(out.at[pl.ds(at, e)], out.at[pl.ds(at, e)], t3s.at[g, d - 1], t3r.at[g, d - 1], (dp, pz[d - 1])) for d in range(1, Z)]
        for copy in copies:
            copy.start()
        return copies

    def after4(g):
        out, _, at, _, _, q, _ = where_out(g)
        copy = remote(out.at[pl.ds(at, q)], out.at[pl.ds(at, q)], t2s.at[g], t2r.at[g], (dp, groups[g][4][1]))
        copy.start()
        return [copy]

    def after5(g):
        out, at, _, _, h, _, _ = where_out(g)
        copy = remote(out.at[pl.ds(at, h)], out.at[pl.ds(at, h)], t1s.at[g], t1r.at[g], (dp, groups[g][3][1]))
        copy.start()
        return [copy]

    def small0():
        sm[...] = jnp.zeros_like(sm)
        for index, r, j, row in small_pieces():
            sm[row:row + 1] = smalls[index][r:r + 1, j * STATE:(j + 1) * STATE]
        copies = [remote(sm, smr.at[i], ms.at[i], mr.at[i], (o, seq)) for i, o in enumerate(others)]
        for copy in copies:
            copy.start()
        return copies

    def small_step(src, extra, dst, slots, peers):
        v = src[...]
        for ref in extra:
            v = v + ref
        dst[0] = v
        copies = [remote(dst.at[0], dst.at[1 + k], ms.at[slots + k], mr.at[slots + k], (dp, q)) for k, q in enumerate(peers)]
        for copy in copies:
            copy.start()
        return copies

    stages = [after0, after1, after2, after3, after4, after5]
    flying = [begin0(g) for g in range(G)]
    tiny = small0()
    done = []
    for stage_at, stage in enumerate(stages):
        for g in range(G):
            for copy in flying[g]:
                copy.wait_recv()
            done += flying[g]
            flying[g] = stage(g)
        if stage_at < 4:
            for copy in tiny:
                copy.wait_recv()
            done += tiny
            if stage_at == 0:
                tiny = small_step(sm, [smr[i] for i in range(ndp - 1)], smx, ndp - 1, [px])
            elif stage_at == 1:
                tiny = small_step(smx.at[0], [smx[1]], smy, ndp, [py])
            elif stage_at == 2:
                tiny = small_step(smy.at[0], [smy[1]], smz, ndp + 1, pz)
            else:
                v = None
                for k in range(Z):
                    slot = lax.rem(z - k + Z, Z)
                    v = smz[slot] if v is None else v + smz[slot]
                small_out[...] = v
    for g in range(G):
        for copy in flying[g]:
            copy.wait_recv()
        done += flying[g]
    for copy in done:
        copy.wait_send()


def all_reduce(ndp, nseq, parts, smalls):
    Z = nseq // PLANE
    counts = tuple(a.shape[1] for a in parts)
    total = sum(counts)
    G = 2 * len(counts)
    V = pltpu.VMEM
    vmem = pl.BlockSpec(memory_space=pltpu.VMEM)
    u = lambda *lead: tuple(lead) + (UNIT, STATE)
    nsm = ndp - 1 + 2 + Z - 1
    small = (SMALL_ROWS, STATE)
    return pl.pallas_call(
        functools.partial(reduce_body, ndp, nseq, counts),
        in_specs=[vmem] * (len(parts) + len(smalls)),
        out_specs=[vmem] * (len(parts) + 1),
        out_shape=[jax.ShapeDtypeStruct(a.shape[1:], BF16) for a in parts] + [jax.ShapeDtypeStruct(small, F32)],
        scratch_shapes=[
            V(u(ndp - 1, total), BF16), V(u(total // 2), F32), V(u(total // 2), BF16), V(u(total // 2), BF16),
            V(u(total // 4), F32), V(u(total // 4), BF16), V(u(total // 4), BF16), V(u(total // 4), BF16),
            V(u(Z - 1, total // 4 // Z), BF16),
            V(small, F32), V((ndp - 1,) + small, F32), V((2,) + small, F32), V((2,) + small, F32), V((Z,) + small, F32),
            DMA((G, ndp - 1)), DMA((G, ndp - 1)), DMA((G,)), DMA((G,)), DMA((G,)), DMA((G,)), DMA((G, Z - 1)), DMA((G, Z - 1)),
            DMA((G, Z - 1)), DMA((G, Z - 1)), DMA((G,)), DMA((G,)), DMA((G,)), DMA((G,)), DMA((nsm,)), DMA((nsm,))],
        compiler_params=pltpu.CompilerParams(collective_id=4, has_side_effects=True, vmem_limit_bytes=VMEM_LIMIT),
        name="reduce_gradients",
    )(*parts, *smalls)


def unpack_body(g1_ref, g2_ref, sm_ref, gin_ref, gout_ref, cw_ref, cb_ref, ng_ref, og_ref, head_ref):
    R = gin_ref.shape[1]
    U = R // UNIT
    tile = lambda ref, j: ref[j * U:(j + 1) * U].astype(F32).reshape(R, STATE)
    eye = jnp.where(iota((STATE, STATE), 0) == iota((STATE, STATE), 1), 1.0, 0.0).astype(BF16)
    turned = lambda ref, j: mm_nt(eye, ref[j * U:(j + 1) * U].reshape(R, STATE))
    for j in range(12):
        gin_ref[j * STATE:(j + 1) * STATE] = turned(g1_ref, j)
    for j in range(14):
        gin_ref[DIN + j * STATE:DIN + (j + 1) * STATE] = turned(g2_ref, j)
    gin_ref[DIN + XBC:] = turned(g2_ref, 14)[:HEADS]
    for half in range(2):
        for j in range(D // STATE):
            gout_ref[half * R:(half + 1) * R, j * STATE:(j + 1) * STATE] = tile(g1_ref, 12 + half * 6 + j)
    outs = {0: cw_ref, 1: cb_ref, 2: ng_ref, 3: og_ref}
    low, high = iota((1, STATE), 1) < HEAD_DIM, iota((1, STATE), 1)
    lane = iota((1, STATE), 1)
    skip = jnp.zeros((1, STATE), F32)
    for index, r, j, row in small_pieces():
        v = sm_ref[row:row + 1]
        if index in outs:
            outs[index][r:r + 1, j * STATE:(j + 1) * STATE] = v
        elif index == 4:
            left = jnp.sum(jnp.where(low, v, 0.0), axis=1, keepdims=True)
            right = jnp.sum(jnp.where(low, 0.0, v), axis=1, keepdims=True)
            skip = skip + jnp.where(lane == 2 * j, left, 0.0) + jnp.where(lane == 2 * j + 1, right, 0.0)
        else:
            head_ref[r + 1:r + 2] = v
    head_ref[0:1] = skip


def unpack(g1, g2, sm, R):
    vmem = pl.BlockSpec(memory_space=pltpu.VMEM)
    sds = lambda *s: jax.ShapeDtypeStruct(s, F32)
    return pl.pallas_call(
        unpack_body,
        in_specs=[vmem] * 3,
        out_specs=[vmem] * 7,
        out_shape=[sds(PROJ, R), sds(2 * R, D), sds(CONV, XBC), sds(1, XBC), sds(1, D), sds(1, DIN), sds(3, STATE)],
        compiler_params=pltpu.CompilerParams(vmem_limit_bytes=VMEM_LIMIT),
        name="unpack_gradients",
    )(g1, g2, sm)


def per_device(ndp, nseq, tokens, in_weight, out_weight, conv_weight, conv_bias, norm_gain, out_gain, skip_gain, rate_code, step_code, cotangent):
    micro, groups, T, _ = tokens.shape
    M = micro * groups
    tok = tokens.reshape(M, T, D)
    cot = cotangent.reshape(M, T, D)
    seq = lax.axis_index("seq")
    turned = in_weight.T
    steps = jnp.pad(turned[DIN + XBC:], ((0, STATE - HEADS), (0, 0)))
    if in_weight.shape[0] % STATE == 0:
        w, ws, wo, halo = open_kernel(ndp, nseq, turned, steps, out_weight, tok)
    else:
        w, ws, wo = [lax.all_gather(v, "dp", axis=at, tiled=True) for v, at in ((turned[:DIN + XBC], 1), (steps, 1), (out_weight, 0))]
        halo = lax.ppermute(tok[:, T - HALO:], "seq", [(i, i + 1) for i in range(nseq - 1)])
    pad = lambda v: jnp.pad(v.astype(F32), (0, STATE - HEADS))
    hp = jnp.stack([pad(rate_code), pad(step_code), pad(skip_gain)])
    ng, og, cb = norm_gain[None], out_gain[None], conv_bias[None]
    gate, cin, cout, bc, ypart, info, sl, sdev, totals = k1(tok, halo, w, ws, conv_weight, cb, ng, hp)
    start = exchange(nseq, False, sdev, totals, KIND)
    mixed, dgate, dy, r, gl, gdev, ogr, gt1 = k2(tok, cot, ng, og, wo, hp, gate, ypart, bc, info, sl, start, ndp, units(ndp, nseq, 24))
    later = exchange(nseq, True, gdev, totals, KIND)
    dcin, tail, head, dstep, gcw, gcb, gskip, ghead = k3(hp, conv_weight, cin, cout, bc, info, sl, start, dy, r, gl, later)
    nxt = lax.ppermute(head, "seq", [(i, i - 1) for i in range(1, nseq)])
    gtok, ngr, gt2 = k4(tok, cot, ng, w, ws, conv_weight, dgate, dcin, dstep, tail, nxt, ndp, units(ndp, nseq, 16))
    g1, g2, sm = all_reduce(ndp, nseq, (gt1, gt2), (gcw, gcb, ngr, ogr, gskip, ghead))
    g_in, g_out, cwg, cbg, ngg, ogg, heads = unpack(g1, g2, sm, D // ndp)
    return (mixed.reshape(tokens.shape), gtok.reshape(tokens.shape), g_in.T, g_out, cwg, cbg[0], ngg[0], ogg[0],
            heads[0, :HEADS], heads[1, :HEADS], heads[2, :HEADS])


def units(ndp, nseq, tiles):
    need, step = tiles * (D // ndp // UNIT), 2 * nseq
    return -(-need // step) * step


def solution(mesh):
    rows, split = P("dp", None), P(None, "dp", "seq", None)
    return jax.shard_map(
        functools.partial(per_device, mesh.shape["dp"], mesh.shape["seq"]),
        mesh=mesh,
        in_specs=(split, rows, rows) + (P(),) * 7 + (split,),
        out_specs=(split, split, rows, rows) + (P(),) * 7,
        check_vma=False,
    )
```

time: 1280 us -> 393 us (0.31)
  waiting for transfers between devices: 476 us -> 5.6 us
  matrix products: 391 us -> 0 us
  Pallas kernels: 0 us -> 369 us
  other arithmetic: 133 us -> 5.77 us
  blocking collectives: 119 us -> 0 us
  local copies, waits for them, and re-layouts: 124 us -> 7.86 us
  between operations: 15.9 us -> 0.71 us
    dot_general x42 -> x0, matrix products: 391 us -> none  [the longest x4 73.7 us: fold_states(): return jnp.einsum('cgh,cghpn->ghpn', weights, piece, precision=HIGH)]
    pallas_call x0 -> x9, Pallas kernels: none -> 369 us  [the longest x4 169 us: call(): pl.pallas_call(body, grid=grid, in_specs=[s for s, _ in ins], out_specs=[...]
    all_gather x6 -> x0, waiting for transfers between devices: 271 us -> none  [the longest x2 131 us: per_device(): lax.all_gather(d_start[None], 'seq', axis=0, tiled=True)]
    psum x1 -> x0, waiting for transfers between devices: 182 us -> none  [per_device(): share_in, share_out = lax.psum((rows_in, rows_out), 'seq')]
    all_gather x2 -> x0, blocking collectives: 73.3 us -> none  [per_device(): totals = lax.all_gather(block_total[None], 'seq', axis=0, tiled=True)]
    reduce_sum x16 -> x0, other arithmetic: 50.7 us -> none  [the longest x2 16.4 us: per_device(): grad_conv_bias = grad_conv_bias + jnp.sum(d_conv, axis=(0, 1))]
    psum x1 -> x0, blocking collectives: 45.6 us -> none  [per_device(): lax.psum((grad_conv_weight, grad_conv_bias, grad_norm_gain, grad_out_gain...]
    mul x10 -> x0, other arithmetic: 44.6 us -> none  [the longest x1 15.9 us: per_device(): mixed_in = jax.nn.silu(conv_out)]
  transfers between devices with their start and end apart: 13 -> 1, of which waited for: 7 -> 1; matrix products, arithmetic and copies ran while one was open for 42% -> 0% of each run, Pallas kernels for 0% -> 0%
where the time goes in v1:
time: 393 us; the launch traced here: 390 us
  Pallas kernels  369 us (94%)
  local copies, waits for them, and re-layouts  7.86 us (2%)
  other arithmetic  5.77 us (1%)
  waiting for transfers between devices  5.6 us (1%)
    pallas_call x4, Pallas kernels, call(): pl.pallas_call(body, grid=grid, in_specs=[s for s, _ in ins], out_specs=[...  169 us
    pallas_call x1, Pallas kernels, all_reduce(): pl.pallas_call(functools.partial(reduce_body, ndp, nseq, counts), in_spec...  110 us
    pallas_call x2, Pallas kernels, exchange(): pl.pallas_call(functools.partial(states_body, nseq, upward), in_specs=[vm...  65 us
    pallas_call x1, Pallas kernels, open_kernel(): pl.pallas_call(functools.partial(open_body, ndp, nseq), in_specs=[vmem] *...  18.5 us
  transfers between devices with their start and end apart: 1, of which 1 were waited for; matrix products, arithmetic and copies ran while one was open for 0% of the time, Pallas kernels for 0%

profile of v1, /device:TPU:0, one launch (start us, length us, event | category | flops | bytes accessed | tf_op | source)
XLA Modules:
  0.0 390.2 jit_solution(7408770629697521255)
XLA Ops:
  0.6 0.7 convert_element_type.12
  1.3 0.7 convert_element_type.13
  2.0 1.3 broadcast_in_dim.9.ng_ref
  3.2 1.3 broadcast_in_dim.10.og_ref
  4.5 1.3 broadcast_in_dim.11.cb_ref
  5.8 0.7 slice.16
  6.5 0.7 pad_bitcast_fusion
  7.2 0.6 pad.14.ws_ref
  8.4 18.5 %gather_weights.1 = (bf16[3328,768]{1,0:T(8,128)(2,1)}, bf16[128,768]{1,0:T(8,128)(2,1)}, bf16[1536,768]{1,0:T(8,128)(2,1)}, bf16[2,16,768]{2,1,0:T(8,128)(2,1)}) custom-call(bf16[3352,384]{1,0:T(8,128)(2,1)} %bitcast.29, bf16[128,384]{1,0:T(8,128)(2,1)} %pad.14.ws_ref, bf16[768,768]{1,0:T(8,128)(2,1)} %wout_ref.1, bf16[2,512,768]{2,1,0:T(8,128)(2,1)} %bitcast.22), custom_call_target="tpu_custom_call" | custom-call | tf_op jit(solution)/shard_map/gather_weights/pallas_call | solution.py:632
  26.9 41.2 %forward_local.1 = (f32[2,512,1536]{2,1,0:T(8,128)}, f32[2,528,1792]{2,1,0:T(8,128)}, f32[2,512,1792]{2,1,0:T(8,128)}, f32[2,512,256]{2,1,0:T(8,128)}, f32[2,512...) custom-call(bf16[2,512,768]{2,1,0:T(8,128)(2,1)} %bitcast.23, ...), custom_call_target="tpu_custom_call" | custom-call | tf_op jit(solution)/shard_map/forward_local/pallas_call | solution.py:224
  68.1 23.5 %states_earlier.1.start_ref = bf16[2,128,1536]{2,1,0:T(8,128)(2,1)} custom-call(f32[2,128,1536]{2,1,0:T(8,128)} %get-tuple-element.62.s_ref, f32[2,128]{1,0:T(2,128)} %get-tuple-element.63.tot_ref), custom_call_target="tpu_custom_call" | custom-call | tf_op jit(solution)/shard_map/states_earlier/pallas_call | solution.py:725
  91.6 57.9 %gate_and_out.1 = (bf16[2,512,768]{2,1,0:T(8,128)(2,1)}, bf16[2,512,1536]{2,1,0:T(8,128)(2,1)}, bf16[2,512,1536]{2,1,0:T(8,128)(2,1)}, f32[2,512,128]{2,1,0:T(8,...) custom-call(bf16[2,512,768]{2,1,0:T(8,128)(2,1)} %bitcast.24, ...), custom_call_target="tpu_custom_call" | custom-call | tf_op jit(solution)/shard_map/gate_and_out/pallas_call | solution.py:224
  149.5 41.5 %states_later.1.later_ref = bf16[2,128,1536]{2,1,0:T(8,128)(2,1)} custom-call(f32[2,128,1536]{2,1,0:T(8,128)} %get-tuple-element.71.s_ref, f32[2,128]{1,0:T(2,128)} %get-tuple-element.63.tot_ref), custom_call_target="tpu_custom_call" | custom-call | tf_op jit(solution)/shard_map/states_later/pallas_call | solution.py:725
  191.0 47.7 %scan_backward.1 = (bf16[2,512,1792]{2,1,0:T(8,128)(2,1)}, f32[2,16,1792]{2,1,0:T(8,128)}, f32[2,8,1792]{2,1,0:T(8,128)}, bf16[2,512,128]{2,1,0:T(8,128)(2,1)}, ...) custom-call(f32[3,128]{1,0:T(4,128)} %pad_maximum_fusion.hp_ref, ...), custom_call_target="tpu_custom_call" | custom-call | tf_op jit(solution)/shard_map/scan_backward/pallas_call | solution.py:224
  238.7 1.3 collective-permute-start
  240.0 5.6 %collective-permute-done.next_ref = f32[2,8,1792]{2,1,0:T(8,128)S(1)} collective-permute-done((f32[2,8,1792]{2,1,0:T(8,128)}, f32[2,8,1792]{2,1,0:T(8,128)S(1)}, u32[]{:S(2)}, u32[]{:S(2)}) %collective-permute-start) | collective-permute-done | bytes 114720 | tf_op jit(solution)/shard_map/ppermute | solution.py:1022
  245.6 0.7 copy-done
  246.3 22.2 %projection_backward.1 = (bf16[2,512,768]{2,1,0:T(8,128)(2,1)}, f32[1,768]{1,0:T(1,128)}, bf16[2,384,16,128]{3,2,1,0:T(8,128)(2,1)}) custom-call(bf16[2,512,768]{2,1,0:T(8,128)(2,1)} %bitcast.25, bf16[2,512,768]{2,1,0:T(8,128)(2,1)} %bitcast.27, f32[1,768]{1,0:T(1,128)} %broadcast_in_dim.9.ng_ref, bf16[3328,768]{1,0:T(8,128)(2,1)} %get-tuple-element.55.w_ref, ...), custom_call_target="tpu_custom_call" | custom-call | tf_op jit(solution)/shard_map/projection_backward/pallas_call | solution.py:224
  268.4 110.0 %reduce_gradients.1 = (bf16[576,16,128]{2,1,0:T(8,128)(2,1)}, bf16[384,16,128]{2,1,0:T(8,128)(2,1)}, f32[104,128]{1,0:T(8,128)}) custom-call(bf16[2,576,16,128]{3,2,1,0:T(8,128)(2,1)} %get-tuple-element.77.refs_0_, bf16[2,384,16,128]{3,2,1,0:T(8,128)(2,1)} %get-tuple-element.78.refs_1_, f32[4,1792]{1,0:T(4,128)} %get-tuple-element.79.refs_2_, ...), custom_call_target="tpu_custom_call" | custom-call | tf_op jit(solution)/shard_map/reduce_gradients/pallas_call | solution.py:940
  378.5 6.5 %unpack_gradients.1 = (f32[3352,384]{1,0:T(8,128)}, f32[768,768]{1,0:T(8,128)}, f32[4,1792]{1,0:T(4,128)}, f32[1,1792]{1,0:T(1,128)}, f32[1,768]{1,0:T(1,128)}, /*index=5*/f32[1,1536]{1,0:T(1,128)}, f32[3,128]{1,0:T(4,128)}) custom-call(bf16[576,16,128]{2,1,0:T(8,128)(2,1)} %get-tuple-element.85.g1_ref, bf16[384,16,128]{2,1,0:T(8,128)(2,1)} %get-tuple-element.86.g2_ref, ...), custom_call_target="tpu_custom_call" | custom-call | tf_op jit(solution)/shard_map/unpack_gradients/pallas_call | solution.py:991
  385.0 1.3 slice_bitcast_fusion
  386.3 1.3 reduce.1
  387.6 1.3 reduce
  388.9 1.3 reduce.2
  (3 shorter events, 0.6 us)
Async XLA Ops:
  238.7 6.9 %collective-permute-start = (f32[2,8,1792]{2,1,0:T(8,128)}, f32[2,8,1792]{2,1,0:T(8,128)S(1)}, u32[]{:S(2)}, u32[]{:S(2)}) collective-permute-start(f32[2,8,1792]{2,1,0:T(8,128)} %get-tuple-element.75), channel_id=1, source_target_pairs={{1,0},{2,1},{3,2},{4,3},{5,4},{6,5},{7,6},{8,7},{9,8},{10,9},{11,1... | collective-permute-start | bytes 344072 | tf_op jit(solution)/shard_map/ppermute | solution.py:1022
  245.6 0.7 copy-start

commit v2 on v1

v2 whole, which is shorter than its diff:
```python
import functools

import jax
import jax.numpy as jnp
from jax import lax
from jax.experimental import pallas as pl
from jax.experimental.pallas import tpu as pltpu
from jax.sharding import PartitionSpec as P

D = 768
DIN = 1536
HEADS = 24
HEAD_DIM = 64
STATE = 128
CONV = 4
XBC = 1792
PROJ = 3352
EPS = 1e-05
LOG2E = 1.4426950408889634
CHUNK = 128
TILE = 256
HALO = 16
UNIT = 16
KIND = jnp.float32
F32 = jnp.float32
BF16 = jnp.bfloat16
VMEM_LIMIT = 62 * 1024 * 1024


def mm(a, b):
    return lax.dot_general(a, b, (((1,), (0,)), ((), ())), preferred_element_type=F32)


def mm_nt(a, b):
    return lax.dot_general(a, b, (((1,), (1,)), ((), ())), preferred_element_type=F32)


def mm_tn(a, b):
    return lax.dot_general(a, b, (((0,), (0,)), ((), ())), preferred_element_type=F32)


def split2(v):
    hi = v.astype(BF16)
    return hi, (v - hi.astype(F32)).astype(BF16)


def split3(v):
    hi = v.astype(BF16)
    rest = v - hi.astype(F32)
    mid = rest.astype(BF16)
    return hi, mid, (rest - mid.astype(F32)).astype(BF16)


def iota(shape, dim):
    return lax.broadcasted_iota(jnp.int32, shape, dim)


def spread_matrix(start, width):
    head = iota((2 * STATE, width), 0) & (STATE - 1)
    column = (iota((2 * STATE, width), 1) + start) >> 6
    return jnp.where(head == column, 1.0, 0.0).astype(BF16)


def gather_matrix():
    return jnp.where((iota((DIN, STATE), 0) >> 6) == iota((DIN, STATE), 1), 1.0, 0.0).astype(BF16)


def spread(v, matrix):
    return mm(jnp.concatenate(split2(v), axis=1), matrix)


def head_sums(v, matrix, parts=3):
    pieces = split3(v) if parts == 3 else split2(v)
    total = mm(pieces[0], matrix)
    for piece in pieces[1:]:
        total = total + mm(piece, matrix)
    return total


def fine_nt(a, b):
    ah, al = split2(a)
    bh, bl = split2(b)
    return mm_nt(jnp.concatenate([ah, ah, al], axis=1), jnp.concatenate([bh, bl, bh], axis=1))


def halves(v):
    return jnp.concatenate(split2(v), axis=0)


def triangle(upper):
    row, column = iota((CHUNK, CHUNK), 0), iota((CHUNK, CHUNK), 1)
    keep = column >= row if upper else column <= row
    return jnp.where(keep, 1.0, 0.0).astype(BF16)


def tri_sum(tri, v):
    return mm(jnp.concatenate([tri] * 3, axis=1), jnp.concatenate(split3(v), axis=0))


def head_params(hp_ref):
    hp = hp_ref[...]
    decay = -jnp.exp(-4.0 + 0.25 * hp[0:1])
    bias = -9.0 + 0.25 * hp[1:2]
    return decay, bias, hp


def sigmoid(v):
    return 1.0 / (1.0 + jnp.exp(-v))


def norm_rows(tok, gain):
    src = tok.astype(F32)
    scale = lax.rsqrt(jnp.mean(src * src, axis=-1, keepdims=True) + EPS)
    return src, scale, (src * scale * gain).astype(BF16)


def pair_masks():
    low = iota((CHUNK, STATE), 1) < HEAD_DIM
    return low, jnp.logical_not(low)


def doubled(v):
    low, high = pair_masks()
    wide = v.astype(F32)
    return jnp.concatenate([jnp.where(low, wide, 0.0).astype(BF16), jnp.where(high, wide, 0.0).astype(BF16)], axis=0)


def k1_body(tok_ref, halo_ref, w_ref, ws_ref, cw_ref, cb_ref, ng_ref, hp_ref,
            gate_ref, cin_ref, cout_ref, bc_ref, ypart_ref, info_ref, sl_ref, sdev_ref, tot_ref, cum_ref, chalo_ref,
            cpad, an, u, ub, dt2, tw2):
    T = tok_ref.shape[1]
    NC = T // CHUNK
    decay, bias, hp = head_params(hp_ref)
    decay2 = decay * LOG2E
    gain = ng_ref[...]
    first = lax.axis_index("seq") == 0
    an[0:HALO] = jnp.where(first, 0.0, norm_rows(halo_ref[0], gain)[2].astype(F32)).astype(BF16)
    an[HALO:] = norm_rows(tok_ref[0], gain)[2]
    arg = mm_nt(an[HALO:], ws_ref[...]) + bias
    dt = jnp.maximum(arg, 0.0) + jnp.log1p(jnp.exp(-jnp.abs(arg)))
    info_ref[0, 0] = arg
    info_ref[0, 1] = dt
    dt2[...] = jnp.concatenate(split2(dt), axis=1)
    tri = triangle(False)
    total = jnp.zeros((1, STATE), F32)
    ends = []
    for c in range(NC):
        rows = slice(c * CHUNK, (c + 1) * CHUNK)
        lc = tri_sum(tri, dt[rows] * decay2)
        info_ref[0, 2, rows] = lc
        ends.append(lc[CHUNK - 1:CHUNK])
        total = total + ends[-1]
        tw2[rows] = jnp.concatenate(split2(jnp.exp2(lc[CHUNK - 1:CHUNK] - lc)), axis=1)

    tot_ref[pl.ds(pl.program_id(0), 1)] = total
    before, after = jnp.zeros((1, STATE), F32), jnp.zeros((1, STATE), F32)
    for c in range(NC + 1):
        cum_ref[0, 0, c:c + 1] = before
        cum_ref[0, 1, NC - c:NC - c + 1] = after
        if c < NC:
            before, after = before + ends[c], after + ends[NC - 1 - c]

    @pl.loop(0, DIN // TILE)
    def _(j):
        cols = pl.ds(pl.multiple_of(j * TILE, TILE), TILE)
        gate_ref[0, :, cols] = mm_nt(an[HALO:], w_ref[cols, :])

    def conv_tile(j, cols):
        wcols = pl.ds(pl.multiple_of(DIN + j * TILE, TILE), TILE)
        raw = mm_nt(an[...], w_ref[wcols, :])
        cpad[...] = raw
        cin_ref[0, :, cols] = raw[HALO:]
        chalo_ref[0, :, cols] = raw[:HALO]
        out = cb_ref[:, cols]
        for k in range(CONV):
            out = out + cw_ref[k:k + 1, cols] * cpad[HALO - CONV + 1 + k:HALO - CONV + 1 + k + T]
        cout_ref[0, :, cols] = out
        return out * sigmoid(out)

    @pl.loop(0, DIN // TILE)
    def _(j):
        cols = pl.ds(pl.multiple_of(j * TILE, TILE), TILE)
        x = conv_tile(j, cols)
        matrix = spread_matrix(j * TILE, TILE)
        ux = x * mm(dt2[...], matrix)
        u[:, cols] = ux.astype(BF16)
        hi, lo = split2(ux * mm(tw2[...], matrix))
        for c in range(NC):
            rows = slice(c * CHUNK, (c + 1) * CHUNK)
            ub[c, 0:CHUNK, cols] = hi[rows]
            ub[c, CHUNK:, cols] = lo[rows]
        skip_tile = spread(jnp.broadcast_to(hp[2:3], (8, STATE)), matrix)[0:1]
        ypart_ref[0, :, cols] = x * skip_tile

    bc_ref[0] = conv_tile(DIN // TILE, pl.ds(DIN, TILE))

    causal = iota((CHUNK, CHUNK), 0) >= iota((CHUNK, CHUNK), 1)
    sdev_ref[0] = jnp.zeros((STATE, DIN), F32)

    @pl.loop(0, NC)
    def _(c):
        rows = pl.ds(pl.multiple_of(c * CHUNK, CHUNK), CHUNK)
        b = bc_ref[0, rows, 0:STATE]
        gram = jnp.where(causal, fine_nt(bc_ref[0, rows, STATE:2 * STATE], b), 0.0)
        b16 = b.astype(BF16)
        lc = info_ref[0, 2, rows]
        lct = lc.T
        sl_ref[0, c] = sdev_ref[0]
        total = jnp.exp2(jnp.broadcast_to(lc[CHUNK - 1:CHUNK], (8, STATE)))
        keep = spread(total, spread_matrix(0, DIN))[0:1]
        sdev_ref[0] = keep * sdev_ref[0] + mm_tn(jnp.concatenate([b16, b16], axis=0), ub[c])
        for p in range(HEADS // 2):
            cols = slice(p * STATE, (p + 1) * STATE)
            mixes = []
            for h in (2 * p, 2 * p + 1):
                gap = lc[:, h:h + 1] - lct[h:h + 1, :]
                mixes.append((gram * jnp.exp2(jnp.minimum(gap, 0.0))).astype(BF16))
            ypart_ref[0, rows, cols] = ypart_ref[0, rows, cols] + mm(jnp.concatenate(mixes, axis=1), doubled(u[rows, cols]))

    sl_ref[0, NC] = sdev_ref[0]


def whole(shape):
    rank = len(shape)
    return pl.BlockSpec(shape, lambda m: (0,) * rank)


def per_micro(shape, buffers=None):
    rank = len(shape)
    mode = None if buffers is None else pl.Buffered(buffers)
    return pl.BlockSpec((1,) + shape, lambda m: (m,) + (0,) * rank, pipeline_mode=mode)


def call(body, grid, ins, outs, scratch, name):
    return pl.pallas_call(
        body,
        grid=grid,
        in_specs=[s for s, _ in ins],
        out_specs=[s for s, _ in outs],
        out_shape=[o for _, o in outs],
        scratch_shapes=scratch,
        compiler_params=pltpu.CompilerParams(vmem_limit_bytes=VMEM_LIMIT, dimension_semantics=("arbitrary",) * len(grid)),
        name=name,
    )(*[a for _, a in ins])


def k1(tok, halo, w, ws, cw, cb, ng, hp):
    M, T, _ = tok.shape
    NC = T // CHUNK
    S = lambda shape, dt: (per_micro(shape), jax.ShapeDtypeStruct((M,) + shape, dt))
    return call(
        k1_body, (M,),
        [(per_micro((T, D)), tok), (per_micro((HALO, D)), halo), (whole(w.shape), w), (whole(ws.shape), ws),
         (whole(cw.shape), cw), (whole(cb.shape), cb), (whole(ng.shape), ng), (whole(hp.shape), hp)],
        [S((T, DIN), F32), S((T, XBC), F32), S((T, XBC), F32), S((T, 2 * STATE), F32), S((T, DIN), F32),
         S((3, T, STATE), F32), S((NC + 1, STATE, DIN), F32), S((STATE, DIN), F32),
         (whole((M, STATE)), jax.ShapeDtypeStruct((M, STATE), F32)), S((2, NC + 1, STATE), F32), S((HALO, XBC), F32)],
        [pltpu.VMEM((HALO + T, TILE), F32), pltpu.VMEM((HALO + T, D), BF16), pltpu.VMEM((T, DIN), BF16), pltpu.VMEM((NC, 2 * CHUNK, DIN), BF16),
         pltpu.VMEM((T, 2 * STATE), BF16), pltpu.VMEM((T, 2 * STATE), BF16)],
        "forward_local",
    )


def chunk_totals(info_ref, NC):
    return [info_ref[0, 2, (c + 1) * CHUNK - 1:(c + 1) * CHUNK] for c in range(NC)]


def product_sum(left, right, cols):
    total = mm(left[0], right[0, :, cols])
    for m in range(1, left.shape[0]):
        total = total + mm(left[m], right[m, :, cols])
    return total


def put_tile(gtile_ref, d, tile, part):
    count = part.shape[0] // UNIT
    gtile_ref[d, pl.ds(tile * count, count)] = part.reshape(count, UNIT, STATE)


def clear_tiles(gtile_ref, rows, tiles):
    low, high = tiles * (rows // UNIT), gtile_ref.shape[1]
    if high > low:
        gtile_ref[:, low:] = jnp.zeros((gtile_ref.shape[0], high - low, UNIT, STATE), BF16)


def weight_tiles(gtile_ref, rows, left, right, count):
    @pl.loop(0, count)
    def _(j):
        part = product_sum(left, right, pl.ds(pl.multiple_of(j * STATE, STATE), STATE)).astype(BF16)
        for d in range(gtile_ref.shape[0]):
            put_tile(gtile_ref, d, j, part[d * rows:(d + 1) * rows])


def k2_body(tok_ref, cot_ref, ng_ref, og_ref, wo_ref, hp_ref, gate_ref, ypart_ref, bc_ref, info_ref, sl_ref, start_ref,
            mixed_ref, dgate_ref, dy_ref, r_ref, gl_ref, gdev_ref, ogr_ref, branch_t_ref, norm_t_ref,
            y, dbr, branch, oscale):
    m = pl.program_id(0)
    T = tok_ref.shape[1]
    NC = T // CHUNK
    matrix = spread_matrix(0, DIN)
    gather = gather_matrix()
    src, _, normed = norm_rows(tok_ref[0], ng_ref[...])
    norm_t_ref[0] = normed.T

    @pl.when(m == 0)
    def _():
        ogr_ref[...] = jnp.zeros_like(ogr_ref)

    totals = chunk_totals(info_ref, NC)
    before = jnp.zeros((1, STATE), F32)
    for c in range(NC):
        rows = slice(c * CHUNK, (c + 1) * CHUNK)
        keep = spread(jnp.exp2(jnp.broadcast_to(before, (8, STATE))), matrix)[0:1]
        before = before + totals[c]
        state = halves(sl_ref[0, c].astype(F32) + keep * start_ref[0].astype(F32))
        c16 = bc_ref[0, rows, STATE:2 * STATE].astype(BF16)
        lift = spread(jnp.exp2(info_ref[0, 2, rows]), matrix)
        yc = ypart_ref[0, rows] + lift * mm(jnp.concatenate([c16, c16], axis=1), state)
        y[rows] = yc
        g = gate_ref[0, rows]
        gated = yc * (g * sigmoid(g))
        scale = lax.rsqrt(jnp.mean(gated * gated, axis=-1, keepdims=True) + EPS)
        oscale[rows] = jnp.broadcast_to(scale, (CHUNK, STATE))
        branch[rows] = (gated * scale * og_ref[...]).astype(BF16)
    branch_t_ref[0] = branch[...].T
    cot = cot_ref[0]
    for j in range(D // TILE):
        cols = slice(j * TILE, (j + 1) * TILE)
        mixed_ref[0, :, cols] = (tok_ref[0, :, cols].astype(F32) + mm(branch[...], wo_ref[:, cols])).astype(BF16)

    @pl.loop(0, DIN // TILE)
    def _(j):
        cols = pl.ds(pl.multiple_of(j * TILE, TILE), TILE)
        dbr[:, cols] = mm_nt(cot, wo_ref[cols, :])

    gdev_ref[0] = jnp.zeros((STATE, DIN), F32)

    @pl.loop(0, NC)
    def _(i):
        c = NC - 1 - i
        rows = pl.ds(pl.multiple_of(c * CHUNK, CHUNK), CHUNK)
        g = gate_ref[0, rows]
        yc = y[rows]
        db = dbr[rows]
        scale = oscale[rows][:, 0:1]
        sig = sigmoid(g)
        act = g * sig
        gated = yc * act
        unit = gated * scale
        ogr_ref[...] += jnp.sum(db * unit, axis=0, keepdims=True)
        e = db * og_ref[...]
        mean = jnp.mean(e * unit, axis=-1, keepdims=True)
        dgated = scale * (e - unit * mean)
        dgate_ref[0, rows] = (dgated * yc * (sig * (1.0 + g * (1.0 - sig)))).astype(BF16)
        high, low = split2(dgated * act)
        dyf = high.astype(F32) + low.astype(F32)
        dy_ref[0, rows] = dyf
        r_ref[0, rows] = head_sums(dyf * yc, gather)
        lc = info_ref[0, 2, rows]
        lifted = halves(dyf * spread(jnp.exp2(lc), matrix))
        c16 = bc_ref[0, rows, STATE:2 * STATE].astype(BF16)
        gl_ref[0, c] = gdev_ref[0]
        total = jnp.exp2(jnp.broadcast_to(lc[CHUNK - 1:CHUNK], (8, STATE)))
        keep = spread(total, matrix)[0:1]
        gdev_ref[0] = keep * gdev_ref[0] + mm_tn(jnp.concatenate([c16, c16], axis=0), lifted)


def early_grads_body(norm_t, branch_t, dgate, cot, gtile_ref):
    dp = gtile_ref.shape[0]
    rows = D // dp
    weight_tiles(gtile_ref, rows, norm_t, dgate, DIN // STATE)
    clear_tiles(gtile_ref, rows, 24)

    @pl.loop(0, D // STATE)
    def _(j):
        part = product_sum(branch_t, cot, pl.ds(pl.multiple_of(j * STATE, STATE), STATE)).astype(BF16)
        for d in range(dp):
            for half in range(2):
                low = (2 * d + half) * rows
                put_tile(gtile_ref, d, 12 + half * 6 + j, part[low:low + rows])


def early_grads(norm_t, branch_t, dgate, cot, dp, units):
    vmem = pl.BlockSpec(memory_space=pltpu.VMEM)
    return pl.pallas_call(
        early_grads_body,
        in_specs=[vmem] * 4,
        out_specs=vmem,
        out_shape=jax.ShapeDtypeStruct((dp, units, UNIT, STATE), BF16),
        compiler_params=pltpu.CompilerParams(vmem_limit_bytes=VMEM_LIMIT),
        name="early_gradients",
    )(norm_t, branch_t, dgate, cot)


def k2(tok, cot, ng, og, wo, hp, gate, ypart, bc, info, sl, start):
    M, T, _ = tok.shape
    NC = T // CHUNK
    S = lambda shape, dt: (per_micro(shape), jax.ShapeDtypeStruct((M,) + shape, dt))
    W = lambda shape, dt: (whole(shape), jax.ShapeDtypeStruct(shape, dt))
    one = lambda a, n=1: (per_micro(a.shape[1:], n), a)
    all_ = lambda a: (whole(a.shape), a)
    return call(
        k2_body, (M,),
        [one(tok), one(cot), all_(ng), all_(og), all_(wo), all_(hp), one(gate), one(ypart, 1), one(bc), one(info), one(sl), one(start, 1)],
        [S((T, D), BF16), S((T, DIN), BF16), S((T, DIN), F32), S((T, STATE), F32), S((NC, STATE, DIN), F32),
         S((STATE, DIN), F32), W((1, DIN), F32), S((DIN, T), BF16), S((D, T), BF16)],
        [pltpu.VMEM((T, DIN), F32), pltpu.VMEM((T, DIN), F32), pltpu.VMEM((T, DIN), BF16), pltpu.VMEM((T, STATE), F32)],
        "gate_and_out",
    )


MESH = pl.DeviceIdType.MESH
PLANE = 4
QUARTER = DIN // PLANE
DMA = pltpu.SemaphoreType.DMA


def places():
    seq = lax.axis_index("seq")
    return lax.axis_index("dp"), seq, lax.rem(seq, PLANE), lax.div(seq, PLANE)


def greet(devices):
    barrier = pltpu.get_barrier_semaphore()
    for device in devices:
        pl.semaphore_signal(barrier, inc=1, device_id=device, device_id_type=MESH)
    pl.semaphore_wait(barrier, len(devices))


def remote(src, dst, send, recv, device):
    return pltpu.make_async_remote_copy(
        src_ref=src, dst_ref=dst, send_sem=send, recv_sem=recv, device_id=device, device_id_type=MESH)


def open_body(ndp, nseq, win_ref, ws_ref, wout_ref, tok_ref, w_ref, wsall_ref, wo_ref, halo_ref, send, recv, hsend, hrecv):
    dp, seq, _, _ = places()
    nxt, prev = lax.rem(seq + 1, nseq), lax.rem(seq + nseq - 1, nseq)
    others = [lax.rem(dp + d, ndp) for d in range(1, ndp)]
    greet([(o, seq) for o in others] + [(dp, nxt), (dp, prev)])
    T = tok_ref.shape[1]
    width, rows = win_ref.shape[1], wout_ref.shape[0]
    columns = pl.ds(pl.multiple_of(dp * width, width), width)
    own_rows = pl.ds(pl.multiple_of(dp * rows, rows), rows)
    moves = [(ws_ref, wsall_ref.at[:, columns]), (win_ref.at[0:DIN + XBC], w_ref.at[:, columns]), (wout_ref, wo_ref.at[own_rows])]
    copies = [remote(tok_ref.at[:, T - HALO:T], halo_ref, hsend, hrecv, (dp, nxt))]
    for i, o in enumerate(others):
        for k, (src, dst) in enumerate(moves):
            copies.append(remote(src, dst, send.at[i, k], recv.at[i, k], (o, seq)))
    for copy in copies:
        copy.start()
    w_ref[:, columns] = win_ref[0:DIN + XBC]
    wsall_ref[:, columns] = ws_ref[...]
    wo_ref[own_rows] = wout_ref[...]
    for copy in copies:
        copy.wait()


def open_kernel(ndp, nseq, win, ws, wout, tok):
    vmem = pl.BlockSpec(memory_space=pltpu.VMEM)
    M = tok.shape[0]
    shape = lambda *s: jax.ShapeDtypeStruct(s, BF16)
    return pl.pallas_call(
        functools.partial(open_body, ndp, nseq),
        in_specs=[vmem] * 3 + [pl.BlockSpec(memory_space=pl.ANY)],
        out_specs=[vmem] * 4,
        out_shape=[shape(DIN + XBC, D), shape(STATE, D), shape(DIN, D), shape(M, HALO, D)],
        scratch_shapes=[DMA((ndp - 1, 3)), DMA((ndp - 1, 3)), DMA, DMA],
        compiler_params=pltpu.CompilerParams(collective_id=1, has_side_effects=True, vmem_limit_bytes=VMEM_LIMIT),
        name="gather_weights",
    )(win, ws, wout, tok)


def states_body(nseq, upward, s_ref, tot_ref, out_ref, stage, got, tots, pre, back, hop, sems, rsems, tsem, trsem, zs, zr, bs, br):
    dp, seq, p, z = places()
    M = s_ref.shape[0]
    Z = nseq // PLANE
    base = z * PLANE
    peers = [lax.rem(p + d, PLANE) for d in range(PLANE)]
    zup, zdown = lax.rem(seq + PLANE, nseq), lax.rem(seq + nseq - PLANE, nseq)
    greet([(dp, base + peers[d]) for d in range(1, PLANE)] + [(dp, zup), (dp, zdown)])
    columns = lambda q: pl.ds(pl.multiple_of(q * QUARTER, QUARTER), QUARTER)
    tots[0] = tot_ref[...]
    tcopies = [remote(tot_ref, tots.at[d], tsem.at[d - 1], trsem.at[d - 1], (dp, base + peers[d])) for d in range(1, PLANE)]
    for copy in tcopies:
        copy.start()
    first = []
    for m in range(M):
        stage[m] = s_ref[m].astype(stage.dtype)
        row = []
        for d in range(1, PLANE):
            copy = remote(stage.at[m, :, columns(peers[d])], got.at[m, d], sems.at[m, d - 1], rsems.at[m, d - 1], (dp, base + peers[d]))
            copy.start()
            row.append(copy)
        first.append(row)
    for copy in tcopies:
        copy.wait()
    shift = peers[0] * QUARTER
    order = list(range(PLANE))[::-1] if upward else list(range(PLANE))
    towards = zdown if upward else zup
    head = (z == Z - 1) if upward else (z == 0)
    tail = (z == 0) if upward else (z == Z - 1)
    last = []
    for m in range(M):
        for copy in first[m]:
            copy.wait_recv()
        matrix = spread_matrix(shift, QUARTER)
        slots = [lax.rem(p - q + PLANE, PLANE) for q in order]
        keep = [spread(jnp.exp2(jnp.broadcast_to(tots[s, m:m + 1], (8, STATE))), matrix)[0:1] for s in slots]

        got[m, 0] = s_ref[m, :, columns(p)].astype(got.dtype)
        link = remote(hop.at[m], pre.at[m], zs.at[m], zr.at[m], (dp, towards))

        @pl.when(head)
        def _():
            pre[m] = jnp.zeros_like(pre[m])

        @pl.when(jnp.logical_not(head))
        def _():
            link.wait_recv()

        run = pre[m].astype(F32)
        for i, q in enumerate(order):
            back[m, slots[i]] = run.astype(back.dtype)
            run = keep[i] * run + got[m, slots[i]].astype(F32)
        hop[m] = run.astype(hop.dtype)

        @pl.when(jnp.logical_not(tail))
        def _():
            link.start()

        for d in range(1, PLANE):
            to = lax.rem(p + PLANE - d, PLANE)
            copy = remote(back.at[m, d], out_ref.at[m, :, columns(p)], bs.at[m, d - 1], br.at[m, d - 1], (dp, base + to))
            copy.start()
            last.append(copy)
        out_ref[m, :, columns(p)] = back[m, 0]
    for row in first:
        for copy in row:
            copy.wait_send()
    for copy in last:
        copy.wait()
    for m in range(M):
        link = remote(hop.at[m], pre.at[m], zs.at[m], zr.at[m], (dp, towards))

        @pl.when(jnp.logical_not(tail))
        def _():
            link.wait_send()


def exchange(nseq, upward, s, tot, kind):
    M = s.shape[0]
    V = pltpu.VMEM
    vmem = pl.BlockSpec(memory_space=pltpu.VMEM)
    quarter = (STATE, QUARTER)
    return pl.pallas_call(
        functools.partial(states_body, nseq, upward),
        in_specs=[vmem] * 2,
        out_specs=vmem,
        out_shape=jax.ShapeDtypeStruct(s.shape, kind),
        scratch_shapes=[V(s.shape, kind), V((M, PLANE) + quarter, kind), V((PLANE,) + tot.shape, F32), V((M,) + quarter, kind),
                        V((M, PLANE) + quarter, kind), V((M,) + quarter, kind),
                        DMA((M, 3)), DMA((M, 3)), DMA((3,)), DMA((3,)), DMA((M,)), DMA((M,)), DMA((M, 3)), DMA((M, 3))],
        compiler_params=pltpu.CompilerParams(collective_id=3 if upward else 2, has_side_effects=True, vmem_limit_bytes=VMEM_LIMIT),
        name="states_later" if upward else "states_earlier",
    )(s, tot)


SMALL = (("cw", CONV, XBC), ("cb", 1, XBC), ("ng", 1, D), ("og", 1, DIN), ("skip", 1, DIN), ("head", 2, STATE))
SMALL_ROWS = 104


def small_pieces():
    row, found = 0, []
    for index, (_, rows, width) in enumerate(SMALL):
        for r in range(rows):
            for j in range(width // STATE):
                found.append((index, r, j, row))
                row += 1
    return found


def strided(count, body):
    step = max(s for s in range(1, 13) if count % s == 0)

    @pl.loop(0, count // step)
    def _(i):
        body(pl.multiple_of(i * step, step), step)


GROUPS = 4


def units(ndp, nseq, tiles):
    need, step = tiles * (D // ndp // UNIT), GROUPS * nseq
    return -(-need // step) * step


def reducer_scratch(ndp, nseq, count):
    Z = nseq // PLANE
    u = lambda n, *lead: tuple(lead) + (n, UNIT, STATE)
    V = pltpu.VMEM
    pairs = [DMA((GROUPS, ndp - 1))] * 2 + [DMA((GROUPS,))] * 4 + [DMA((GROUPS, Z - 1))] * 4 + [DMA((GROUPS,))] * 4
    return [V(u(count, ndp - 1), BF16), V(u(count // 2), F32), V(u(count // 2), BF16), V(u(count // 2), BF16),
            V(u(count // 4), F32), V(u(count // 4), BF16), V(u(count // 4), BF16), V(u(count // 4), BF16),
            V(u(count // 4 // Z, Z - 1), BF16)] + pairs


class Reducer:
    def __init__(self, ndp, nseq, src, out, scratch):
        self.ndp, self.Z = ndp, nseq // PLANE
        self.src, self.out = src, out
        (self.r0, self.w1, self.st1, self.r1, self.w2, self.st2, self.r2, self.st3, self.r3) = scratch[:9]
        self.sems = [(scratch[9 + 2 * k], scratch[10 + 2 * k]) for k in range(7)]
        self.dp, self.seq, self.p, self.z = places()
        x, y = lax.rem(self.p, 2), lax.div(self.p, 2)
        self.others = [lax.rem(self.dp + d, ndp) for d in range(1, ndp)]
        self.pz = [lax.rem(self.z + d, self.Z) * PLANE + self.p for d in range(1, self.Z)]
        sides = ((x, self.seq + 1 - 2 * x), (y, self.seq + 2 - 4 * y))
        self.sides = [sides if g % 2 == 0 else sides[::-1] for g in range(GROUPS)]
        self.size = src.shape[1] // GROUPS
        self.half, self.quarter = self.size // 2, self.size // 4
        self.piece = self.quarter // self.Z

    def partners(self):
        (_, px), (_, py) = self.sides[0]
        return [(o, self.seq) for o in self.others] + [(self.dp, q) for q in (px, py)] + [(self.dp, q) for q in self.pz]

    def copies(self, stage, g):
        sizes, at = self.size, g * self.size
        o1, o2, o3 = g * self.half, g * self.quarter, g * self.piece
        send, recv = self.sems[stage]
        (b1, peer1), (b2, peer2) = self.sides[g]
        half_at = at + b1 * self.half
        quarter_at = half_at + b2 * self.quarter
        piece_at = quarter_at + self.z * self.piece
        if stage == 0:
            return [remote(self.src.at[o, pl.ds(at, sizes)], self.r0.at[i, pl.ds(at, sizes)], send.at[g, i], recv.at[g, i], (o, self.seq))
                    for i, o in enumerate(self.others)]
        if stage == 1:
            span = pl.ds(o1, self.half)
            return [remote(self.st1.at[span], self.r1.at[span], send.at[g], recv.at[g], (self.dp, peer1))]
        if stage == 2:
            span = pl.ds(o2, self.quarter)
            return [remote(self.st2.at[span], self.r2.at[span], send.at[g], recv.at[g], (self.dp, peer2))]
        if stage == 3:
            return [remote(self.st3.at[pl.ds(o2 + lax.rem(self.z + d, self.Z) * self.piece, self.piece)], self.r3.at[d - 1, pl.ds(o3, self.piece)],
                           send.at[g, d - 1], recv.at[g, d - 1], (self.dp, self.pz[d - 1])) for d in range(1, self.Z)]
        if stage == 4:
            span = pl.ds(piece_at, self.piece)
            return [remote(self.out.at[span], self.out.at[span], send.at[g, d - 1], recv.at[g, d - 1], (self.dp, self.pz[d - 1]))
                    for d in range(1, self.Z)]
        span, peer = (pl.ds(quarter_at, self.quarter), peer2) if stage == 5 else (pl.ds(half_at, self.half), peer1)
        return [remote(self.out.at[span], self.out.at[span], send.at[g], recv.at[g], (self.dp, peer))]

    def stage(self, stage, g):
        if stage > 0:
            for copy in self.copies(stage - 1, g):
                copy.wait_recv()
        if stage == 7:
            return
        (b1, _), (b2, _) = self.sides[g]
        at, o1, o2, o3 = g * self.size, g * self.half, g * self.quarter, g * self.piece
        if stage == 1:
            def total(i, c):
                v = self.src[self.dp, pl.ds(at + i, c)].astype(F32)
                for k in range(self.ndp - 1):
                    v = v + self.r0[k, pl.ds(at + i, c)].astype(F32)
                return v

            def body(i, c):
                self.w1[pl.ds(o1 + i, c)] = total(b1 * self.half + i, c)
                self.st1[pl.ds(o1 + i, c)] = total((1 - b1) * self.half + i, c).astype(BF16)
            strided(self.half, body)
        elif stage == 2:
            def body(i, c):
                keep, give = pl.ds(o1 + b2 * self.quarter + i, c), pl.ds(o1 + (1 - b2) * self.quarter + i, c)
                self.w2[pl.ds(o2 + i, c)] = self.w1[keep] + self.r1[keep].astype(F32)
                self.st2[pl.ds(o2 + i, c)] = (self.w1[give] + self.r1[give].astype(F32)).astype(BF16)
            strided(self.quarter, body)
        elif stage == 3:
            def body(i, c):
                span = pl.ds(o2 + i, c)
                v = self.w2[span] + self.r2[span].astype(F32)
                self.w2[span] = v
                self.st3[span] = v.astype(BF16)
            strided(self.quarter, body)
        elif stage == 4:
            v = self.w2[pl.ds(o2 + self.z * self.piece, self.piece)]
            for d in range(self.Z - 1):
                v = v + self.r3[d, pl.ds(o3, self.piece)].astype(F32)
            self.out[pl.ds(at + b1 * self.half + b2 * self.quarter + self.z * self.piece, self.piece)] = v.astype(BF16)
        for copy in self.copies(stage, g):
            copy.start()

    def ticks(self):
        def tick(k):
            if k == 0:
                for g in range(GROUPS):
                    self.stage(0, g)
                return
            for stage, groups in ((k, (0, 1)), (k - 1, (2, 3))):
                if 1 <= stage <= 7:
                    for g in groups:
                        self.stage(stage, g)
        return [functools.partial(tick, k) for k in range(9)]

    def finish(self):
        for stage in range(7):
            for g in range(GROUPS):
                for copy in self.copies(stage, g):
                    copy.wait_send()


def small_scratch(ndp, nseq):
    Z = nseq // PLANE
    V = pltpu.VMEM
    shape = (SMALL_ROWS, STATE)
    count = ndp - 1 + 2 + Z - 1
    return [V((ndp,) + shape, F32), V((2,) + shape, F32), V((2,) + shape, F32), V((Z,) + shape, F32), DMA((count,)), DMA((count,))]


class SmallReducer:
    def __init__(self, ndp, nseq, out, scratch):
        self.out = out
        self.bufs, (self.send, self.recv) = scratch[:4], scratch[4:6]
        dp, seq, p, z = places()
        Z = nseq // PLANE
        x, y = lax.rem(p, 2), lax.div(p, 2)
        self.z, self.Z = z, Z
        self.peers = [[(lax.rem(dp + d, ndp), seq) for d in range(1, ndp)], [(dp, seq + 1 - 2 * x)], [(dp, seq + 2 - 4 * y)],
                      [(dp, lax.rem(z + d, Z) * PLANE + p) for d in range(1, Z)]]
        self.at, self.begun, self.over, self.started = 0, False, False, []

    def send_all(self):
        buf = self.bufs[self.at]
        base = sum(len(q) for q in self.peers[:self.at])
        self.flying = [remote(buf.at[0], buf.at[1 + k], self.send.at[base + k], self.recv.at[base + k], device)
                       for k, device in enumerate(self.peers[self.at])]
        for copy in self.flying:
            copy.start()
        self.started += self.flying

    def begin(self, groups):
        buf = self.bufs[0]
        buf[0] = jnp.zeros(buf.shape[1:], F32)
        for index, r, j, row in small_pieces():
            v = groups[index][0][r:r + 1, j * STATE:(j + 1) * STATE]
            for other in groups[index][1:]:
                v = v + other[r:r + 1, j * STATE:(j + 1) * STATE]
            buf[0, row:row + 1] = v
        self.begun = True
        self.send_all()

    def advance(self):
        if self.over:
            return
        for copy in self.flying:
            copy.wait_recv()
        buf = self.bufs[self.at]
        if self.at < 3:
            v = buf[0]
            for k in range(1, buf.shape[0]):
                v = v + buf[k]
            self.at += 1
            self.bufs[self.at][0] = v
            self.send_all()
            return
        v = None
        for k in range(self.Z):
            piece = buf[lax.rem(self.z - k + self.Z, self.Z)]
            v = piece if v is None else v + piece
        self.out[...] = v
        self.over = True

    def finish(self):
        for copy in self.started:
            copy.wait_send()


def unpack_body(g1_ref, g2_ref, sm_ref, gin_ref, gout_ref, cw_ref, cb_ref, ng_ref, og_ref, head_ref):
    R = gin_ref.shape[1]
    U = R // UNIT
    tile = lambda ref, j: ref[j * U:(j + 1) * U].astype(F32).reshape(R, STATE)
    eye = jnp.where(iota((STATE, STATE), 0) == iota((STATE, STATE), 1), 1.0, 0.0).astype(BF16)
    turned = lambda ref, j: mm_nt(eye, ref[j * U:(j + 1) * U].reshape(R, STATE))
    for j in range(12):
        gin_ref[j * STATE:(j + 1) * STATE] = turned(g1_ref, j)
    for j in range(14):
        gin_ref[DIN + j * STATE:DIN + (j + 1) * STATE] = turned(g2_ref, j)
    gin_ref[DIN + XBC:] = turned(g2_ref, 14)[:HEADS]
    for half in range(2):
        for j in range(D // STATE):
            gout_ref[half * R:(half + 1) * R, j * STATE:(j + 1) * STATE] = tile(g1_ref, 12 + half * 6 + j)
    outs = {0: cw_ref, 1: cb_ref, 2: ng_ref, 3: og_ref}
    low, high = iota((1, STATE), 1) < HEAD_DIM, iota((1, STATE), 1)
    lane = iota((1, STATE), 1)
    skip = jnp.zeros((1, STATE), F32)
    for index, r, j, row in small_pieces():
        v = sm_ref[row:row + 1]
        if index in outs:
            outs[index][r:r + 1, j * STATE:(j + 1) * STATE] = v
        elif index == 4:
            left = jnp.sum(jnp.where(low, v, 0.0), axis=1, keepdims=True)
            right = jnp.sum(jnp.where(low, 0.0, v), axis=1, keepdims=True)
            skip = skip + jnp.where(lane == 2 * j, left, 0.0) + jnp.where(lane == 2 * j + 1, right, 0.0)
        else:
            head_ref[r + 1:r + 2] = v
    head_ref[0:1] = skip


def unpack(g1, g2, sm, R):
    vmem = pl.BlockSpec(memory_space=pltpu.VMEM)
    sds = lambda *s: jax.ShapeDtypeStruct(s, F32)
    return pl.pallas_call(
        unpack_body,
        in_specs=[vmem] * 3,
        out_specs=[vmem] * 7,
        out_shape=[sds(PROJ, R), sds(2 * R, D), sds(CONV, XBC), sds(1, XBC), sds(1, D), sds(1, DIN), sds(3, STATE)],
        compiler_params=pltpu.CompilerParams(vmem_limit_bytes=VMEM_LIMIT),
        name="unpack_gradients",
    )(g1, g2, sm)
def k3_body(ndp, nseq, hp_ref, cw_ref, chalo_ref, cum_ref, cin_ref, cout_ref, bc_ref, info_ref, sl_ref, sl_next_ref, start_ref, dy_ref, r_ref,
            gl_ref, later_ref, g1_ref,
            dcin_ref, tail_ref, head_ref, dstep_ref, gcw_ref, gcb_ref, gskip_ref, ghead_ref, sum1_ref,
            dconv, w, xdu, ub, dyl, dgt, dt_x, tail_x, bg, landing, *comm):
    m, i = pl.program_id(0), pl.program_id(1)
    NC = pl.num_programs(1)
    c = NC - 1 - i
    step = m * NC + i
    steps = pl.num_programs(0) * NC
    reducer = Reducer(ndp, nseq, g1_ref, landing, comm)
    ticks = reducer.ticks()
    for k, tick in enumerate(ticks[:-1]):

        @pl.when(step == k)
        def _():
            if k == 0:
                greet(reducer.partners())
            tick()

    decay, _, hp = head_params(hp_ref)
    matrix = spread_matrix(0, DIN)
    gather = gather_matrix()
    skip = spread(jnp.broadcast_to(hp[2:3], (8, STATE)), matrix)[0:1]

    @pl.when(step == 0)
    def _():
        gcw_ref[...] = jnp.zeros_like(gcw_ref)
        gcb_ref[...] = jnp.zeros_like(gcb_ref)
        gskip_ref[...] = jnp.zeros_like(gskip_ref)
        ghead_ref[...] = jnp.zeros_like(ghead_ref)

    @pl.when(i == 0)
    def _():
        dconv[CHUNK:] = jnp.zeros((8, XBC), F32)

    @pl.when(i > 0)
    def _():
        dconv[CHUNK:] = dconv[0:8]

    tri_up = triangle(True)
    b32 = bc_ref[0, :, 0:STATE]
    c32 = bc_ref[0, :, STATE:2 * STATE]
    keeps_st = iota((CHUNK, CHUNK), 0) <= iota((CHUNK, CHUNK), 1)
    gram_t = jnp.where(keeps_st, fine_nt(c32, b32).T, 0.0)
    b, cc = b32.astype(BF16), c32.astype(BF16)
    lc = info_ref[0, 2]
    lct = lc.T
    dt = info_ref[0, 1]
    dt_x[...] = spread(dt, matrix)
    tail_x[...] = spread(jnp.exp2(lc[CHUNK - 1:CHUNK] - lc), matrix)
    dyl[...] = (dy_ref[0] * spread(jnp.exp2(lc), matrix)).astype(BF16)
    wide8 = lambda v: spread(jnp.exp2(jnp.broadcast_to(v, (8, STATE))), matrix)[0:1]
    gc = gl_ref[0, 0] + wide8(cum_ref[0, 1, pl.ds(c + 1, 1)]) * later_ref[0].astype(F32)
    s_in = sl_ref[0, 0] + wide8(cum_ref[0, 0, pl.ds(c, 1)]) * start_ref[0].astype(F32)
    s_out = sl_next_ref[0, 0] + wide8(cum_ref[0, 0, pl.ds(c + 1, 1)]) * start_ref[0].astype(F32)
    gc2 = halves(gc)
    gcb16 = gc2[0:STATE]
    bnd = head_sums(jnp.broadcast_to(jnp.sum(gc * s_out, axis=0, keepdims=True), (8, DIN)), gather)[0:1]
    bg[...] = mm(jnp.concatenate([b, b], axis=1), gc2)
    dgt[...] = jnp.zeros((CHUNK, CHUNK), F32)
    for p in range(HEADS // 2):
        cols = slice(p * STATE, (p + 1) * STATE)
        v = cout_ref[0, :, cols]
        sig = sigmoid(v)
        x = v * sig
        dtx, tlx = dt_x[:, cols], tail_x[:, cols]
        ux = x * dtx
        u16 = ux.astype(BF16)
        ub[:, cols] = (ux * tlx).astype(BF16)
        dyf = dy_ref[0, :, cols]
        dy_high, dy_low = split2(dyf)
        dy2 = doubled(dy_high)
        decays, mixes = [], []
        for h in (2 * p, 2 * p + 1):
            gap = lct[h:h + 1, :] - lc[:, h:h + 1]
            e = jnp.exp2(jnp.minimum(gap, 0.0))
            decays.append(e)
            mixes.append((gram_t * e).astype(BF16))
        mix = jnp.concatenate(mixes, axis=1)
        du = mm(mix, dy2) + mm(mix, doubled(dy_low))
        dmix = mm_nt(u16, dy2)
        dgt[...] = dgt[...] + (dmix[:, :CHUNK] * decays[0] + dmix[:, CHUNK:] * decays[1])
        du_state = tlx * bg[:, cols]
        sk = skip[:, cols]
        dyx = dyf * x
        gskip_ref[:, cols] = gskip_ref[:, cols] + jnp.sum(dyx, axis=0, keepdims=True)
        w[:, cols] = dyx * sk + u16.astype(F32) * du + ux * du_state
        du = du + du_state
        xdu[:, cols] = x * du
        dx = dtx * du + sk * dyf
        dconv[0:CHUNK, cols] = dx * (sig * (1.0 + v * (1.0 - sig)))
    dg16 = jnp.where(keeps_st, dgt[...], 0.0).astype(BF16)
    db = mm(dg16, cc) + mm_nt(ub[...], gcb16)
    dc = mm_tn(dg16, b) + mm_nt(dyl[...], s_in.astype(BF16))
    v = cout_ref[0, :, DIN:XBC]
    sig = sigmoid(v)
    dconv[0:CHUNK, DIN:XBC] = jnp.concatenate([db, dc], axis=1) * (sig * (1.0 + v * (1.0 - sig)))
    dl = r_ref[0] - head_sums(w[...], gather)
    da = bnd + tri_sum(tri_up, dl)
    d_dt = head_sums(xdu[...], gather, 2) + da * decay
    dstep = d_dt * sigmoid(info_ref[0, 0])
    dstep_ref[0] = dstep.astype(BF16)
    ghead_ref[0:1] = ghead_ref[0:1] + decay * jnp.sum(da * dt, axis=0, keepdims=True)
    ghead_ref[1:2] = ghead_ref[1:2] + jnp.sum(dstep, axis=0, keepdims=True)

    @pl.loop(0, XBC // TILE)
    def _(j):
        cols = pl.ds(pl.multiple_of(j * TILE, TILE), TILE)
        gcb_ref[:, cols] = gcb_ref[:, cols] + jnp.sum(dconv[0:CHUNK, cols], axis=0, keepdims=True)
        own = cin_ref[0, :, cols]
        total = None
        for k in range(CONV):
            ahead = dconv[CONV - 1 - k:CONV - 1 - k + CHUNK, cols]
            gcw_ref[k:k + 1, cols] = gcw_ref[k:k + 1, cols] + jnp.sum(own * ahead, axis=0, keepdims=True)
            term = cw_ref[k:k + 1, cols] * ahead
            total = term if total is None else total + term
        dcin_ref[0, :, cols] = total.astype(BF16)

        @pl.when(i == 0)
        def _():
            tail_ref[0, :, cols] = total[CHUNK - HALO:]

    @pl.when(i == NC - 1)
    def _():
        head_ref[0] = dconv[0:8]
        for k in range(CONV - 1):
            for n in range(CONV - 1 - k):
                low = HALO - CONV + 1 + k + n
                gcw_ref[k:k + 1] = gcw_ref[k:k + 1] + chalo_ref[0, low:low + 1] * dconv[n:n + 1]

    @pl.when(step == steps - 1)
    def _():
        for tick in ticks[-1:]:
            tick()
        reducer.finish()

        def body(at, c):
            sum1_ref[pl.ds(at, c)] = landing[pl.ds(at, c)]
        strided(landing.shape[0], body)


def k3(ndp, nseq, hp, cw, chalo, cum, cin, cout, bc, info, sl, start, dy, r, gl, later, g1):
    M, T, _ = cout.shape
    NC = T // CHUNK
    at = lambda m, i: NC - 1 - i
    const = lambda a: (pl.BlockSpec(a.shape, lambda m, i: (0,) * a.ndim), a)
    micro = lambda a: (pl.BlockSpec((1,) + a.shape[1:], lambda m, i: (m,) + (0,) * (a.ndim - 1)), a)
    chunk = lambda a: (pl.BlockSpec((1, CHUNK) + a.shape[2:], lambda m, i: (m, at(m, i), 0)), a)
    entry = lambda a, ahead: (pl.BlockSpec((1, 1) + a.shape[2:], lambda m, i: (m, at(m, i) + ahead, 0, 0)), a)
    inner = (pl.BlockSpec((1, 3, CHUNK, STATE), lambda m, i: (m, 0, at(m, i), 0)), info)
    sds = jax.ShapeDtypeStruct
    C = lambda width, dt: (pl.BlockSpec((1, CHUNK, width), lambda m, i: (m, at(m, i), 0)), sds((M, T, width), dt))
    S = lambda rows: (pl.BlockSpec((1, rows, XBC), lambda m, i: (m, 0, 0)), sds((M, rows, XBC), F32))
    W = lambda shape, dt: (pl.BlockSpec(shape, lambda m, i: (0,) * len(shape)), sds(shape, dt))
    V = pltpu.VMEM
    ins = [const(hp), const(cw), micro(chalo), micro(cum), chunk(cin), chunk(cout), chunk(bc), inner, entry(sl, 0), entry(sl, 1), micro(start),
           chunk(dy), chunk(r), entry(gl, 0), micro(later), const(g1)]
    outs = [C(XBC, BF16), S(HALO), S(8), C(STATE, BF16), W((CONV, XBC), F32), W((1, XBC), F32), W((1, DIN), F32), W((2, STATE), F32),
            W(g1.shape[1:], BF16)]
    return pl.pallas_call(
        functools.partial(k3_body, ndp, nseq),
        grid=(M, NC),
        in_specs=[b for b, _ in ins],
        out_specs=[b for b, _ in outs],
        out_shape=[o for _, o in outs],
        scratch_shapes=[V((CHUNK + 8, XBC), F32), V((CHUNK, DIN), F32), V((CHUNK, DIN), F32), V((CHUNK, DIN), BF16), V((CHUNK, DIN), BF16),
                        V((CHUNK, CHUNK), F32), V((CHUNK, DIN), F32), V((CHUNK, DIN), F32), V((CHUNK, DIN), F32), V(g1.shape[1:], BF16)] + reducer_scratch(ndp, nseq, g1.shape[1]),
        compiler_params=pltpu.CompilerParams(vmem_limit_bytes=VMEM_LIMIT, dimension_semantics=("arbitrary",) * 2, collective_id=4,
                                             has_side_effects=True),
        name="scan_backward",
    )(*[a for _, a in ins])


def k4_body(ndp, nseq, M, tok_ref, cot_ref, ng_ref, w_ref, ws_ref, cw_ref, dgate_ref, dcin_ref, dstep_ref, tail_ref, head_ref, *refs):
    smalls, rest = refs[:5], refs[5:]
    gtok_ref, sum2_ref, small_out, g2, nxt, dc, norm_t, ngr, hsem, hrsem = rest[:10]
    count = len(reducer_scratch(ndp, nseq, g2.shape[1]))
    reducer = Reducer(ndp, nseq, g2, sum2_ref, rest[10:10 + count])
    tiny = SmallReducer(ndp, nseq, small_out, rest[10 + count:])
    T = tok_ref.shape[1]
    dp, seq, _, _ = places()
    following, prev = lax.rem(seq + 1, nseq), lax.rem(seq + nseq - 1, nseq)
    greet(reducer.partners() + [(dp, following), (dp, prev)])
    halo = remote(head_ref, nxt, hsem, hrsem, (dp, prev))
    halo.start()
    rows = D // ndp
    for m in range(M):
        norm_t[m] = norm_rows(tok_ref[m], ng_ref[...])[2].T
        dc[m, 0:T - HALO, 0:XBC] = dcin_ref[m, 0:T - HALO]
        dc[m, :, XBC:] = dstep_ref[m]
    clear_tiles(g2, rows, 15)
    halo.wait()
    last = seq == nseq - 1
    row = iota((HALO, XBC), 0)
    for m in range(M):
        tail = tail_ref[m]
        for s in range(CONV - 1):
            extra = jnp.zeros((1, XBC), F32)
            for k in range(s + 1):
                extra = extra + cw_ref[k:k + 1] * nxt[m, s - k:s - k + 1]
            tail = tail + jnp.where(jnp.logical_and(row == HALO - CONV + 1 + s, jnp.logical_not(last)), extra, 0.0)
        dc[m, T - HALO:T, 0:XBC] = tail.astype(BF16)
    weight_tiles(g2, rows, norm_t, dc, 15)
    ngr[...] = jnp.zeros_like(ngr)
    ticks = reducer.ticks()

    def backward(m, part):
        if part < D // TILE:
            cols = slice(part * TILE, (part + 1) * TILE)
            dn[:, cols] = (mm(dgate_ref[m], w_ref[0:DIN, cols]) + mm(dc[m, :, 0:XBC], w_ref[DIN:DIN + XBC, cols])
                           + mm(dstep_ref[m], ws_ref[:, cols]))
        else:
            src, scale, _ = norm_rows(tok_ref[m], ng_ref[...])
            unit = src * scale
            d_normed = dn[...]
            ngr[...] += jnp.sum(d_normed * unit, axis=0, keepdims=True)
            f = d_normed * ng_ref[...]
            mean = jnp.mean(f * unit, axis=-1, keepdims=True)
            gtok_ref[m] = (cot_ref[m].astype(F32) + scale * (f - unit * mean)).astype(BF16)

    dn = rest[-1]
    parts = [(m, part) for m in range(M) for part in range(D // TILE + 1)]
    per = -(-len(parts) // (len(ticks) - 2))
    ticks[0]()
    for k, tick in enumerate(ticks[1:]):
        for m, part in parts[:per]:
            backward(m, part)
        parts = parts[per:]
        tick()
        if not parts and not tiny.begun:
            tiny.begin([[r[...] for r in group] for group in small_groups(smalls, ngr, M)])
        elif tiny.begun:
            tiny.advance()
    while not tiny.over:
        tiny.advance()
    tiny.finish()
    reducer.finish()


def small_groups(smalls, ngr, M):
    gcw, gcb, gskip, ghead = smalls[:4]
    return [[gcw], [gcb], [ngr], list(smalls[4:4 + 1]), [gskip], [ghead]]


def k4(ndp, nseq, tok, cot, ng, w, ws, cw, dgate, dcin, dstep, tail, head, gcw, gcb, gskip, ghead, ogr):
    M, T, _ = tok.shape
    V = pltpu.VMEM
    sds = jax.ShapeDtypeStruct
    vmem = pl.BlockSpec(memory_space=pltpu.VMEM)
    count = units(ndp, nseq, 15)
    args = (tok, cot, ng, w, ws, cw, dgate, dcin, dstep, tail, head, gcw, gcb, gskip, ghead, ogr)
    return pl.pallas_call(
        functools.partial(k4_body, ndp, nseq, M),
        in_specs=[vmem] * len(args),
        out_specs=[vmem] * 3,
        out_shape=[sds((M, T, D), BF16), sds((count, UNIT, STATE), BF16), sds((SMALL_ROWS, STATE), F32)],
        scratch_shapes=[V((ndp, count, UNIT, STATE), BF16), V(head.shape, F32), V((M, T, XBC + STATE), BF16), V((M, D, T), BF16), V((1, D), F32),
                        DMA, DMA] + reducer_scratch(ndp, nseq, count) + small_scratch(ndp, nseq) + [V((T, D), F32)],
        compiler_params=pltpu.CompilerParams(collective_id=5, has_side_effects=True, vmem_limit_bytes=VMEM_LIMIT),
        name="projection_backward",
    )(*args)


def per_device(ndp, nseq, tokens, in_weight, out_weight, conv_weight, conv_bias, norm_gain, out_gain, skip_gain, rate_code, step_code, cotangent):
    micro, groups, T, _ = tokens.shape
    M = micro * groups
    tok = tokens.reshape(M, T, D)
    cot = cotangent.reshape(M, T, D)
    seq = lax.axis_index("seq")
    turned = in_weight.T
    steps = jnp.pad(turned[DIN + XBC:], ((0, STATE - HEADS), (0, 0)))
    if in_weight.shape[0] % STATE == 0:
        w, ws, wo, halo = open_kernel(ndp, nseq, turned, steps, out_weight, tok)
    else:
        w, ws, wo = [lax.all_gather(v, "dp", axis=at, tiled=True) for v, at in ((turned[:DIN + XBC], 1), (steps, 1), (out_weight, 0))]
        halo = lax.ppermute(tok[:, T - HALO:], "seq", [(i, i + 1) for i in range(nseq - 1)])
    pad = lambda v: jnp.pad(v.astype(F32), (0, STATE - HEADS))
    hp = jnp.stack([pad(rate_code), pad(step_code), pad(skip_gain)])
    ng, og, cb = norm_gain[None], out_gain[None], conv_bias[None]
    gate, cin, cout, bc, ypart, info, sl, sdev, totals, cum, chalo = k1(tok, halo, w, ws, conv_weight, cb, ng, hp)
    start = exchange(nseq, False, sdev, totals, KIND)
    mixed, dgate, dy, r, gl, gdev, ogr, branch_t, norm_t = k2(tok, cot, ng, og, wo, hp, gate, ypart, bc, info, sl, start)
    g1 = early_grads(norm_t, branch_t, dgate, cot, ndp, units(ndp, nseq, 24))
    later = exchange(nseq, True, gdev, totals, KIND)
    dcin, tail, head, dstep, gcw, gcb, gskip, ghead, sum1 = k3(
        ndp, nseq, hp, conv_weight, chalo, cum, cin, cout, bc, info, sl, start, dy, r, gl, later, g1)
    gtok, sum2, sm = k4(ndp, nseq, tok, cot, ng, w, ws, conv_weight, dgate, dcin, dstep, tail, head, gcw, gcb, gskip, ghead, ogr)
    g_in, g_out, cwg, cbg, ngg, ogg, heads = unpack(sum1, sum2, sm, D // ndp)
    return (mixed.reshape(tokens.shape), gtok.reshape(tokens.shape), g_in.T, g_out, cwg, cbg[0], ngg[0], ogg[0],
            heads[0, :HEADS], heads[1, :HEADS], heads[2, :HEADS])


def solution(mesh):
    rows, split = P("dp", None), P(None, "dp", "seq", None)
    return jax.shard_map(
        functools.partial(per_device, mesh.shape["dp"], mesh.shape["seq"]),
        mesh=mesh,
        in_specs=(split, rows, rows) + (P(),) * 7 + (split,),
        out_specs=(split, split, rows, rows) + (P(),) * 7,
        check_vma=False,
    )
```

time: 393 us -> 387 us (0.985)
  waiting for transfers between devices: 5.6 us -> 0 us
    pallas_call x4 -> x2, Pallas kernels: 169 us -> 88.3 us  [call(): pl.pallas_call(body, grid=grid, in_specs=[s for s, _ in ins], out_specs=[...]
    pallas_call x1 -> x3, Pallas kernels: 110 us -> 162 us  [the longest x1 72.4 us: k3(): pl.pallas_call(functools.partial(k3_body, ndp, nseq), grid=(M, NC), in_sp...]
    pallas_call x2, Pallas kernels: 65 us -> 96.7 us  [exchange(): pl.pallas_call(functools.partial(states_body, nseq, upward), in_specs=[vm...]
    ppermute x1 -> x0, waiting for transfers between devices: 5.6 us -> none  [per_device(): nxt = lax.ppermute(head, 'seq', [(i, i - 1) for i in range(1, nseq)])]
  transfers between devices with their start and end apart: 1 -> 0, of which waited for: 1 -> 0; matrix products, arithmetic and copies ran while one was open for 0% -> 0% of each run, Pallas kernels for 0% -> 0%
where the time goes in v2:
time: 387 us
  Pallas kernels  372 us (96%)
  local copies, waits for them, and re-layouts  8.35 us (2%)
  other arithmetic  5.82 us (2%)
    pallas_call x2, Pallas kernels, exchange(): pl.pallas_call(functools.partial(states_body, nseq, upward), in_specs=[vm...  96.7 us
    pallas_call x2, Pallas kernels, call(): pl.pallas_call(body, grid=grid, in_specs=[s for s, _ in ins], out_specs=[...  88.3 us
    pallas_call x1, Pallas kernels, k3(): pl.pallas_call(functools.partial(k3_body, ndp, nseq), grid=(M, NC), in_sp...  72.4 us
    pallas_call x1, Pallas kernels, k4(): pl.pallas_call(functools.partial(k4_body, ndp, nseq, M), in_specs=[vmem]...  70.7 us
    pallas_call x1, Pallas kernels, early_grads(): pl.pallas_call(early_grads_body, in_specs=[vmem] * 4, out_specs=vmem, out...  18.7 us
    pallas_call x1, Pallas kernels, open_kernel(): pl.pallas_call(functools.partial(open_body, ndp, nseq), in_specs=[vmem] *...  18.4 us

profile of v2, /device:TPU:0, one launch (start us, length us, event | category | flops | bytes accessed | tf_op | source)
XLA Modules:
  0.0 386.8 jit_solution(11757944484360111242)
XLA Ops:
  0.6 0.7 convert_element_type.12
  1.3 0.7 convert_element_type.13
  2.0 0.7 pad_bitcast_fusion
  2.6 0.6 pad_maximum_fusion.hp_ref
  3.2 1.3 broadcast_in_dim.9.ng_ref
  4.5 1.3 broadcast_in_dim.10.og_ref
  5.8 1.3 broadcast_in_dim.11.cb_ref
  7.1 0.7 slice.16
  7.8 0.7 pad.14.ws_ref
  8.5 18.4 %gather_weights.1 = (bf16[3328,768]{1,0:T(8,128)(2,1)}, bf16[128,768]{1,0:T(8,128)(2,1)}, bf16[1536,768]{1,0:T(8,128)(2,1)}, bf16[2,16,768]{2,1,0:T(8,128)(2,1)}) custom-call(bf16[3352,384]{1,0:T(8,128)(2,1)} %bitcast.30, bf16[128,384]{1,0:T(8,128)(2,1)} %pad.14.ws_ref, bf16[768,768]{1,0:T(8,128)(2,1)} %wout_ref.1, bf16[2,512,768]{2,1,0:T(8,128)(2,1)} %bitcast.22), custom_call_target="tpu_custom_call" | custom-call | tf_op jit(solution)/shard_map/gather_weights/pallas_call | solution.py:462
  26.9 41.2 %forward_local.1 = (f32[2,512,1536]{2,1,0:T(8,128)}, f32[2,512,1792]{2,1,0:T(8,128)}, f32[2,512,1792]{2,1,0:T(8,128)}, f32[2,512,256]{2,1,0:T(8,128)}, f32[2,512...) custom-call(bf16[2,512,768]{2,1,0:T(8,128)(2,1)} %bitcast.23, ...), custom_call_target="tpu_custom_call" | custom-call | tf_op jit(solution)/shard_map/forward_local/pallas_call | solution.py:235
  68.1 40.6 %states_earlier.1.start_ref = f32[2,128,1536]{2,1,0:T(8,128)} custom-call(f32[2,128,1536]{2,1,0:T(8,128)} %get-tuple-element.63.s_ref, f32[2,128]{1,0:T(2,128)} %get-tuple-element.64.tot_ref), custom_call_target="tpu_custom_call" | custom-call | tf_op jit(solution)/shard_map/states_earlier/pallas_call | solution.py:555
  108.7 47.2 %gate_and_out.1 = (bf16[2,512,768]{2,1,0:T(8,128)(2,1)}, bf16[2,512,1536]{2,1,0:T(8,128)(2,1)}, f32[2,512,1536]{2,1,0:T(8,128)}, f32[2,512,128]{2,1,0:T(8,128)},...) custom-call(bf16[2,512,768]{2,1,0:T(8,128)(2,1)} %bitcast.24, ...), custom_call_target="tpu_custom_call" | custom-call | tf_op jit(solution)/shard_map/gate_and_out/pallas_call | solution.py:235
  155.9 56.1 %states_later.1.later_ref = f32[2,128,1536]{2,1,0:T(8,128)} custom-call(f32[2,128,1536]{2,1,0:T(8,128)} %get-tuple-element.74.s_ref, f32[2,128]{1,0:T(2,128)} %get-tuple-element.64.tot_ref), custom_call_target="tpu_custom_call" | custom-call | tf_op jit(solution)/shard_map/states_later/pallas_call | solution.py:555
  212.0 18.7 %early_gradients.1.g1_ref = bf16[2,576,16,128]{3,2,1,0:T(8,128)(2,1)} custom-call(bf16[2,768,512]{2,1,0:T(8,128)(2,1)} %get-tuple-element.75.norm_t, bf16[2,1536,512]{2,1,0:T(8,128)(2,1)} %get-tuple-element.76.branch_t, bf16[2,512,1536]{2,1,0:T(8,128)(2,1)} %get-tuple-element.66.dgate.dgate_ref, bf16[2,512,768]{2,1,0:T(8,128)(2,1)} %bitcast.27), custom_call_target="tpu_custom_call" | custom-call | tf_op jit(solution)/shard_map/early_gradients/pallas_call | solution.py:385
  230.7 72.4 %scan_backward.1 = (bf16[2,512,1792]{2,1,0:T(8,128)(2,1)}, f32[2,16,1792]{2,1,0:T(8,128)}, f32[2,8,1792]{2,1,0:T(8,128)}, bf16[2,512,128]{2,1,0:T(8,128)(2,1)}, ...) custom-call(f32[3,128]{1,0:T(4,128)} %pad_maximum_fusion.hp_ref, ...), custom_call_target="tpu_custom_call" | custom-call | tf_op jit(solution)/shard_map/scan_backward/pallas_call | solution.py:981
  303.1 70.7 %projection_backward.1 = (bf16[2,512,768]{2,1,0:T(8,128)(2,1)}, bf16[384,16,128]{2,1,0:T(8,128)(2,1)}, f32[104,128]{1,0:T(8,128)}) custom-call(bf16[2,512,768]{2,1,0:T(8,128)(2,1)} %bitcast.25, bf16[2,512,768]{2,1,0:T(8,128)(2,1)} %bitcast.28, f32[1,768]{1,0:T(1,128)} %broadcast_in_dim.9.ng_ref, bf16[3328,768]{1,0:T(8,128)(2,1)} %get-tuple-element.56.w_ref, ...), custom_call_target="tpu_custom_call" | custom-call | tf_op jit(solution)/shard_map/projection_backward/pallas_call | solution.py:1073
  373.8 0.0 copy-start
  373.8 6.6 %unpack_gradients.1 = (f32[3352,384]{1,0:T(8,128)}, f32[768,768]{1,0:T(8,128)}, f32[4,1792]{1,0:T(4,128)}, f32[1,1792]{1,0:T(1,128)}, f32[1,768]{1,0:T(1,128)}, /*index=5*/f32[1,1536]{1,0:T(1,128)}, f32[3,128]{1,0:T(4,128)}) custom-call(bf16[576,16,128]{2,1,0:T(8,128)(2,1)} %get-tuple-element.87.g1_ref, bf16[384,16,128]{2,1,0:T(8,128)(2,1)} %get-tuple-element.88.g2_ref, ...), custom_call_target="tpu_custom_call" | custom-call | tf_op jit(solution)/shard_map/unpack_gradients/pallas_call | solution.py:814
  380.5 1.3 slice_bitcast_fusion
  381.8 1.3 reduce.1
  383.1 1.3 reduce
  384.4 1.3 reduce.2
  385.7 1.1 copy.25
  (2 shorter events, 0.0 us)
Async XLA Ops:
  373.8 11.9 %copy-start = (bf16[2,512,768]{2,1,0:T(8,128)(2,1)S(1)}, bf16[2,512,768]{2,1,0:T(8,128)(2,1)}, u32[]{:S(2)}) copy-start(bf16[2,512,768]{2,1,0:T(8,128)(2,1)} %get-tuple-element.86) | copy-start | bytes 4718596
